TPU v7x, 256 devices: a whole 4x4x8 slice. The times are simulated.
256 devices in a mesh: lon: 16 (over x, y_lo, core), lat: 16 (over y_hi, z).
Axes of the slice: x: 4, y: 4 (y_hi: 2, y_lo: 2; y = y_hi * 2 + y_lo), z: 8, core: 2. Of those that a mesh axis runs over, the one named last changes fastest.
Arguments:
- tokens: bfloat16 [128, 512, 512], P('lat', 'lon')
- w_qkv: bfloat16 [512, 1536], replicated
- w_proj: bfloat16 [512, 512], replicated, may hold values from -0.25 to 0.25
- w_merge: bfloat16 [2048, 1024], replicated, may hold values from -0.125 to 0.125
- skip_grad: bfloat16 [128, 512, 512], P('lat', 'lon'), may hold values from -6 to 6
- merged_grad: bfloat16 [64, 256, 1024], P('lat', 'lon'), may hold values from -6 to 6
- window_shift: int32 [2], replicated, may hold values from 1 to 7, as said below
Outputs:
- skip_out: bfloat16 [128, 512, 512], P('lat', 'lon')
- merged_out: bfloat16 [64, 256, 1024], P('lat', 'lon')
- input_grad: bfloat16 [128, 512, 512], P('lat', 'lon')
- dw_qkv: float32 [512, 1536], P('lon', 'lat')
- dw_proj: float32 [512, 512], P('lon', 'lat')
- dw_merge: float32 [2048, 1024], P('lon', 'lat')
Inputs may be any that keep to these rules, and one draw needn't show every extreme that they name: window_shift[0] is the latitude offset and window_shift[1] the longitude offset of the windows; one of the two equals 7 and the two differ.
All inputs are finite; a program needn't handle non-finite values.
Results may differ from a plain program's by a relative error of at most 0.029.
The roundings to bfloat16 on the way count: a program that leaves them out, or rounds other values in their place, can miss the bound.
Values may be sent and summed in bfloat16 or wider, within the bound.
A program may use at most 128 MiB of HBM per device.

v0:
```python
import jax
import jax.numpy as jnp
from jax import lax
from jax.sharding import PartitionSpec as P

HEADS = 16
WIN = 8


EPSILON = 1e-05
NEGATIVE = -1e30


def with_halo(shard, sides, width):
    for axis, dim in sides:
        count, length = (lax.axis_size(axis), shard.shape[dim])
        up = [(i, (i + 1) % count) for i in range(count)]
        down = [(j, i) for i, j in up]
        last = lax.slice_in_dim(shard, length - width, length, axis=dim)
        leading = lax.slice_in_dim(shard, 0, width, axis=dim)
        before = lax.ppermute(last, axis, up)
        after = lax.ppermute(leading, axis, down)
        shard = jnp.concatenate([before, shard, after], axis=dim)
    return shard


def normalize(values):
    values = values.astype(jnp.float32)
    center = values - jnp.mean(values, axis=-1, keepdims=True)
    inverse = lax.rsqrt(jnp.mean(center * center, axis=-1, keepdims=True) + EPSILON)
    return (center * inverse, inverse)


def norm_back(grad_in, normed, inverse):
    return inverse * (
        grad_in
        - jnp.mean(grad_in, axis=-1, keepdims=True)
        - normed * jnp.mean(grad_in * normed, axis=-1, keepdims=True)
    )


def merge_cells(grid_in):
    height, across, channels = grid_in.shape
    return (
        grid_in.reshape(height // 2, 2, across // 2, 2, channels)
        .transpose(0, 2, 3, 1, 4)
        .reshape(height // 2, across // 2, 4 * channels)
    )


def split_cells(grid_in):
    height, across, channels = grid_in.shape
    quarter = channels // 4
    return (
        grid_in.reshape(height, across, 2, 2, quarter)
        .transpose(0, 3, 1, 2, 4)
        .reshape(2 * height, 2 * across, quarter)
    )


def to_windows(block_in, extent):
    height, across, channels = block_in.shape
    return (
        block_in.reshape(height // extent, extent, across // extent, extent, channels)
        .transpose(0, 2, 1, 3, 4)
        .reshape(height // extent * (across // extent), extent * extent, channels)
    )


def from_windows(window_in, extent, height, across):
    channels = window_in.shape[-1]
    return (
        window_in.reshape(height // extent, across // extent, extent, extent, channels)
        .transpose(0, 2, 1, 3, 4)
        .reshape(height, across, channels)
    )


def window_mask(row_flags, across):
    grid_flags = jnp.broadcast_to(row_flags[:, None, None], (row_flags.shape[0], across, 1))
    return to_windows(grid_flags, WIN)[:, :, 0]


def split_heads(packed, heads):
    windows, per_window, channels = packed.shape
    model_width = channels // 3
    pieces = packed.reshape(windows, per_window, 3, heads, model_width // heads)
    return (pieces[:, :, 0], pieces[:, :, 1], pieces[:, :, 2])


def weights_of(queries, key_rows, usable):
    factor = queries.shape[-1] ** (-0.5)
    scores = (
        jnp.einsum("nqhd,nkhd->nhqk", queries, key_rows, preferred_element_type=jnp.float32)
        * factor
    )
    scores = jnp.where(usable[:, None, None, :], scores, NEGATIVE)
    highest = jnp.max(scores, axis=-1, keepdims=True)
    raised = jnp.exp(scores - highest)
    return raised / jnp.sum(raised, axis=-1, keepdims=True)


def attend(packed, usable, heads):
    queries, key_rows, value_rows = split_heads(packed, heads)
    probs = weights_of(queries, key_rows, usable)
    rounded = probs.astype(jnp.bfloat16)
    output = jnp.einsum("nhqk,nkhd->nqhd", rounded, value_rows, preferred_element_type=jnp.float32)
    return output.reshape(output.shape[0], output.shape[1], -1).astype(jnp.bfloat16)


def attend_back(packed, usable, upstream, heads):
    queries, key_rows, value_rows = split_heads(packed, heads)
    windows, per_window = (queries.shape[0], queries.shape[1])
    factor = queries.shape[-1] ** (-0.5)
    probs = weights_of(queries, key_rows, usable)
    rounded = probs.astype(jnp.bfloat16)
    grad_out = upstream.reshape(queries.shape)
    prob_grad = jnp.einsum(
        "nqhd,nkhd->nhqk", grad_out, value_rows, preferred_element_type=jnp.float32
    )
    row_total = jnp.sum(probs * prob_grad, axis=-1, keepdims=True)
    score_grad = (probs * (prob_grad - row_total) * factor).astype(jnp.bfloat16)
    query_grad = jnp.einsum(
        "nhqk,nkhd->nqhd", score_grad, key_rows, preferred_element_type=jnp.float32
    )
    key_grad = jnp.einsum(
        "nhqk,nqhd->nkhd", score_grad, queries, preferred_element_type=jnp.float32
    )
    value_grad = jnp.einsum(
        "nhqk,nqhd->nkhd", rounded, grad_out, preferred_element_type=jnp.float32
    )
    return jnp.concatenate(
        [
            query_grad.reshape(windows, per_window, -1),
            key_grad.reshape(windows, per_window, -1),
            value_grad.reshape(windows, per_window, -1),
        ],
        axis=-1,
    )


def on_device(tokens, w_qkv, w_proj, w_merge, skip_grad, merged_grad, window_shift):
    height, across, model_width = tokens.shape
    offset_lat = window_shift[0]
    offset_lon = window_shift[1]
    band_index = lax.axis_index("lat")
    total_rows = height * lax.axis_size("lat")
    global_rows = band_index * height - WIN + jnp.arange(height + 2 * WIN, dtype=jnp.int32)
    row_flags = (global_rows >= 0) & (global_rows < total_rows)
    normed, inverse = normalize(tokens)
    hidden = normed.astype(jnp.bfloat16)
    flat_hidden = hidden.reshape(-1, model_width)
    packed = (
        jnp.dot(flat_hidden, w_qkv, preferred_element_type=jnp.float32)
        .astype(jnp.bfloat16)
        .reshape(height, across, 3 * model_width)
    )
    packed_ext = with_halo(packed, (("lon", 1), ("lat", 0)), WIN)
    packed_ext = jnp.where(row_flags[:, None, None], packed_ext, jnp.zeros_like(packed_ext))
    cut_height = (height // WIN + 1) * WIN
    cut_across = (across // WIN + 1) * WIN
    packed_cut = lax.dynamic_slice(
        packed_ext, (offset_lat, offset_lon, 0), (cut_height, cut_across, 3 * model_width)
    )
    flags_cut = lax.dynamic_slice_in_dim(row_flags, offset_lat, cut_height, 0)
    usable = window_mask(flags_cut, cut_across)
    packed_win = to_windows(packed_cut, WIN)
    output_cut = from_windows(attend(packed_win, usable, HEADS), WIN, cut_height, cut_across)
    attended = lax.dynamic_slice(
        output_cut, (WIN - offset_lat, WIN - offset_lon, 0), (height, across, model_width)
    )
    flat_attended = attended.reshape(-1, model_width)
    summed = tokens.astype(jnp.float32) + jnp.dot(
        flat_attended, w_proj, preferred_element_type=jnp.float32
    ).reshape(height, across, model_width)
    skip_out = summed.astype(jnp.bfloat16)
    merged_in = merge_cells(skip_out)
    merged_normed, merged_inverse = normalize(merged_in)
    merged_hidden = merged_normed.astype(jnp.bfloat16)
    flat_merged = merged_hidden.reshape(-1, 4 * model_width)
    merged_out = (
        jnp.dot(flat_merged, w_merge, preferred_element_type=jnp.float32)
        .astype(jnp.bfloat16)
        .reshape(height // 2, across // 2, -1)
    )
    flat_mgrad = merged_grad.reshape(-1, merged_grad.shape[-1])
    merged_back = jnp.einsum(
        "te,de->td", flat_mgrad, w_merge, preferred_element_type=jnp.float32
    ).reshape(merged_in.shape)
    merged_delta = norm_back(merged_back, merged_normed, merged_inverse)
    total_grad = (skip_grad.astype(jnp.float32) + split_cells(merged_delta)).astype(jnp.bfloat16)
    flat_total = total_grad.reshape(-1, model_width)
    merge_part = jnp.einsum(
        "tc,te->ce", flat_merged, flat_mgrad, preferred_element_type=jnp.float32
    )
    attended_grad = (
        jnp.einsum("te,de->td", flat_total, w_proj, preferred_element_type=jnp.float32)
        .astype(jnp.bfloat16)
        .reshape(height, across, model_width)
    )
    proj_part = jnp.einsum(
        "td,te->de", flat_attended, flat_total, preferred_element_type=jnp.float32
    )
    grad_ext = with_halo(attended_grad, (("lon", 1), ("lat", 0)), WIN)
    grad_ext = jnp.where(row_flags[:, None, None], grad_ext, jnp.zeros_like(grad_ext))
    grad_cut = lax.dynamic_slice(
        grad_ext, (offset_lat, offset_lon, 0), (cut_height, cut_across, model_width)
    )
    packed_back = attend_back(packed_win, usable, to_windows(grad_cut, WIN), HEADS)
    packed_grid = from_windows(packed_back, WIN, cut_height, cut_across)
    packed_grad = lax.dynamic_slice(
        packed_grid, (WIN - offset_lat, WIN - offset_lon, 0), (height, across, 3 * model_width)
    ).astype(jnp.bfloat16)
    flat_pgrad = packed_grad.reshape(-1, 3 * model_width)
    qkv_part = jnp.einsum("td,te->de", flat_hidden, flat_pgrad, preferred_element_type=jnp.float32)
    hidden_grad = jnp.einsum(
        "te,de->td", flat_pgrad, w_qkv, preferred_element_type=jnp.float32
    ).reshape(height, across, model_width)
    input_grad = (total_grad.astype(jnp.float32) + norm_back(hidden_grad, normed, inverse)).astype(
        jnp.bfloat16
    )
    sectioned = (
        lax.psum_scatter(
            qkv_part.astype(jnp.bfloat16), "lon", scatter_dimension=0, tiled=True
        ).astype(jnp.float32),
        lax.psum_scatter(
            proj_part.astype(jnp.bfloat16), "lon", scatter_dimension=0, tiled=True
        ).astype(jnp.float32),
        lax.psum_scatter(
            merge_part.astype(jnp.bfloat16), "lon", scatter_dimension=0, tiled=True
        ).astype(jnp.float32),
    )
    reduced = (
        lax.psum_scatter(
            sectioned[0].astype(jnp.bfloat16), "lat", scatter_dimension=1, tiled=True
        ).astype(jnp.float32),
        lax.psum_scatter(
            sectioned[1].astype(jnp.bfloat16), "lat", scatter_dimension=1, tiled=True
        ).astype(jnp.float32),
        lax.psum_scatter(
            sectioned[2].astype(jnp.bfloat16), "lat", scatter_dimension=1, tiled=True
        ).astype(jnp.float32),
    )
    return (skip_out, merged_out, input_grad, reduced[0], reduced[1], reduced[2])


def solution(mesh):
    in_specs = (
        P("lat", "lon", None),
        P(),
        P(),
        P(),
        P("lat", "lon", None),
        P("lat", "lon", None),
        P(),
    )
    out_specs = (
        P("lat", "lon", None),
        P("lat", "lon", None),
        P("lat", "lon", None),
        P("lon", "lat"),
        P("lon", "lat"),
        P("lon", "lat"),
    )
    return jax.shard_map(
        on_device, mesh=mesh, in_specs=in_specs, out_specs=out_specs, check_vma=False
    )
```

profile of v0, /device:TPU:4, one launch (start us, length us, event | category | flops | bytes accessed | tf_op | source)
XLA Modules:
  0.0 955.5 jit_solution(873214245289849178)
XLA Ops:
  17.7 8.6 collective-permute-start.3
  36.2 15.6 %collective-permute-done.3 = bf16[8,48,1536]{2,1,0:T(8,128)(2,1)} collective-permute-done((bf16[8,48,1536]{2,1,0:T(8,128)(2,1)S(1)}, bf16[8,48,1536]{2,1,0:T(8,128)(2,1)}, u32[]{:S(2)}, u32[]{:S(2)}) %collective-permute-start.3) | collective-permute-done | bytes 1179680 | tf_op jit(solution)/shard_map/ppermute | solution.py:22
  51.8 6.8 collective-permute-done.2
  58.6 5.6 fusion.22
  64.4 7.1 reshape_reshape.7
  71.5 5.6 fusion.84
  77.1 4.6 copy.92
  81.7 4.7 copy.91
  102.6 4.7 convert_element_type.113
  130.8 7.4 collective-permute-done.7
  147.3 4.7 copy.71
  152.0 5.6 convolution_bitcast_fusion.1
  160.9 10.4 %fusion.28 = bf16[10,64,16,32]{1,3,2,0:T(8,128)(2,1)} fusion(f32[10,16,64,64]{2,3,1,0:T(8,128)} %fusion.39, bf16[10,64,1,16,32]{1,4,3,0,2:T(8,128)(2,1)} %copy.92, f32[10,16,64,64]{2,3,1,0:T(8,128)} %copy-done.26, f32[10,16,64]{2,1,0:T(8,128)S(1)} %copy-done.28), kind=kOutput, calls=%fused_computation.35 | convolution fusion | flops 46540864 | bytes 6594560 | tf_op jit(solution)/shard_map/nhqk,nqhd->nkhd/dot_general | solution.py:126
  171.2 4.5 copy.78
  179.8 4.5 copy.75
  184.3 4.8 concatenate.27
  189.1 10.2 %fusion.25 = bf16[10,64,16,32]{1,3,2,0:T(8,128)(2,1)} fusion(f32[10,16,64,64]{2,3,1,0:T(8,128)} %fusion.39, bf16[10,64,1,16,32]{1,4,3,0,2:T(8,128)(2,1)} %copy-done.2, f32[10,16,64,64]{2,3,1,0:T(8,128)} %copy-done.26, f32[10,16,64]{2,1,0:T(8,128)} %copy-done.27), kind=kOutput, calls=%fused_computation.34 | convolution fusion | flops 46540864 | bytes 6594560 | tf_op jit(solution)/shard_map/nhqk,nkhd->nqhd/dot_general | solution.py:123
  199.3 4.4 copy.73
  203.7 5.0 concatenate.26
  222.9 39.0 %reduce-scatter.13.cloned.1.call-done = bf16[32,1536]{1,0:T(8,128)(2,1)} async-done(((bf16[512,1536]{1,0:T(8,128)(2,1)}), bf16[32,1536]{1,0:T(8,128)(2,1)}) %reduce-scatter.13.cloned.1.call-update) | async-done | bytes 98320 | tf_op jit(solution)/shard_map/reduce_scatter | solution.py:223
  265.7 68.7 %reduce-scatter.17.cloned.1.call-done = bf16[128,1024]{1,0:T(8,128)(2,1)} async-done(((bf16[2048,1024]{1,0:T(8,128)(2,1)}), bf16[128,1024]{1,0:T(8,128)(2,1)}) %reduce-scatter.17.cloned.1.call-update) | async-done | bytes 262160 | tf_op jit(solution)/shard_map/reduce_scatter | solution.py:229
  337.2 208.5 %reduce-scatter.21.cloned.1.call-done = bf16[32,32]{1,0:T(8,128)(2,1)} async-done(((bf16[512,32]{1,0:T(8,128)(2,1)}), bf16[32,32]{1,0:T(8,128)(2,1)}) %reduce-scatter.21.cloned.1.call-update) | async-done | bytes 2064
  547.0 201.9 %reduce-scatter.19.cloned.1.call-done = bf16[96,32]{1,0:T(8,128)(2,1)} async-done(((bf16[1536,32]{1,0:T(8,128)(2,1)}), bf16[96,32]{1,0:T(8,128)(2,1)}) %reduce-scatter.19.cloned.1.call-update) | async-done | bytes 6160
  750.4 196.5 %reduce-scatter.23.cloned.1.call-done = bf16[64,128]{1,0:T(8,128)(2,1)} async-done(((bf16[1024,128]{1,0:T(8,128)(2,1)}), bf16[64,128]{1,0:T(8,128)(2,1)}) %reduce-scatter.23.cloned.1.call-update) | async-done | bytes 16400
  (149 shorter events, 94.7 us)
Async XLA Ops:
  7.2 210.3 %reduce-scatter.15.cloned.1.call-start = ((), (), s32[]{:S(2)}) async-start(), calls=%async_computation.7 | async-start | bytes 557056 | tf_op jit(solution)/shard_map/reduce_scatter | solution.py:226
  10.7 6.8 copy-start.11
  10.7 15.8 %copy-start.22 = (s32[2]{0:T(128)S(1)}, s32[2]{0:T(128)}, u32[]{:S(2)}) copy-start(s32[2]{0:T(128)} %param.13) | copy-start | bytes 28
  11.4 6.2 collective-permute-start
  11.4 6.1 collective-permute-start.1
  17.5 9.0 copy-start.14
  17.5 9.0 copy-start.15
  17.7 34.1 %collective-permute-start.3 = (bf16[8,48,1536]{2,1,0:T(8,128)(2,1)S(1)}, bf16[8,48,1536]{2,1,0:T(8,128)(2,1)}, u32[]{:S(2)}, u32[]{:S(2)}) collective-permute-start(bf16[8,48,1536]{2,1,0:T(8,128)(2,1)S(1)} %pad_maximum_fusion), channel_id=1, source_target_pairs={{1,0},{2,1},{3,2},{4,3},{5,4},{6,5},{7,6},{8,7},{9,8},{10,9},{11,1... | collective-permute-start | bytes 3538952 | tf_op jit(solution)/shard_map/ppermute | solution.py:22
  26.2 32.3 %collective-permute-start.2 = (bf16[8,48,1536]{2,1,0:T(8,128)(2,1)S(1)}, bf16[8,48,1536]{2,1,0:T(8,128)(2,1)}, u32[]{:S(2)}, u32[]{:S(2)}) collective-permute-start(bf16[8,48,1536]{2,1,0:T(8,128)(2,1)S(1)} %pad_maximum_fusion), channel_id=1, source_target_pairs={{0,1},{1,2},{2,3},{3,4},{4,5},{5,6},{6,7},{7,8},{8,9},{9,10},{10,1... | collective-permute-start | bytes 3538952 | tf_op jit(solution)/shard_map/ppermute | solution.py:21
  102.6 5.7 copy-start.1
  102.6 5.7 copy-start.8
  120.3 8.3 copy-start.6
  121.8 20.2 %copy-start.25 = (pred[16]{0:T(512)(128)(4,1)S(1)}, pred[16]{0:T(512)(128)(4,1)}, u32[]{:S(2)}) copy-start(pred[16]{0:T(512)(128)(4,1)} %copy-done.24) | copy-start | bytes 52
  121.8 4.7 collective-permute-start.4
  122.2 4.3 collective-permute-start.5
  126.5 11.7 %collective-permute-start.7 = (bf16[8,48,512]{2,1,0:T(8,128)(2,1)S(1)}, bf16[8,48,512]{2,1,0:T(8,128)(2,1)}, u32[]{:S(2)}, u32[]{:S(2)}) collective-permute-start(bf16[8,48,512]{2,1,0:T(8,128)(2,1)S(1)} %pad_maximum_fusion.1), channel_id=1, source_target_pairs={{1,0},{2,1},{3,2},{4,3},{5,4},{6,5},{7,6},{8,7},{9,8},{10,9},{11,1... | collective-permute-start | bytes 1179656 | tf_op jit(solution)/shard_map/ppermute | solution.py:22
  126.6 15.3 %collective-permute-start.6 = (bf16[8,48,512]{2,1,0:T(8,128)(2,1)S(1)}, bf16[8,48,512]{2,1,0:T(8,128)(2,1)}, u32[]{:S(2)}, u32[]{:S(2)}) collective-permute-start(bf16[8,48,512]{2,1,0:T(8,128)(2,1)S(1)} %pad_maximum_fusion.1), channel_id=1, source_target_pairs={{0,1},{1,2},{2,3},{3,4},{4,5},{5,6},{6,7},{7,8},{8,9},{9,10},{10,1... | collective-permute-start | bytes 1179656 | tf_op jit(solution)/shard_map/ppermute | solution.py:21
  130.7 131.1 %reduce-scatter.13.cloned.1.call-start = ((), (), s32[]{:S(2)}) async-start(), calls=%async_computation.6 | async-start | bytes 1671168 | tf_op jit(solution)/shard_map/reduce_scatter | solution.py:223
  213.4 120.9 %reduce-scatter.17.cloned.1.call-start = ((), (), s32[]{:S(2)}) async-start(), calls=%async_computation.8 | async-start | bytes 4456448 | tf_op jit(solution)/shard_map/reduce_scatter | solution.py:229
  216.8 328.8 %reduce-scatter.21.cloned.1.call-start = ((), (), s32[]{:S(2)}) async-start(), calls=%async_computation.10 | async-start | bytes 139264
  219.1 44.7 %copy-start.21 = (f32[8,32]{1,0:T(8,128)S(1)}, f32[8,32]{1,0:T(8,128)}, u32[]{:S(2)}) copy-start(f32[8,32]{1,0:T(8,128)} %copy-done.20) | copy-start | bytes 3076
  219.1 529.9 %reduce-scatter.19.cloned.1.call-start = ((), (), s32[]{:S(2)}) async-start(), calls=%async_computation.9 | async-start | bytes 417792
  222.9 113.3 %copy-start.7 = (bf16[8,32,512]{2,1,0:T(8,128)(2,1)S(1)}, bf16[8,32,512]{2,1,0:T(8,128)(2,1)}, u32[]{:S(2)}) copy-start(bf16[8,32,512]{2,1,0:T(8,128)(2,1)} %copy-done.6) | copy-start | bytes 786436
  263.7 683.2 %reduce-scatter.23.cloned.1.call-start = ((), (), s32[]{:S(2)}) async-start(), calls=%async_computation.11 | async-start | bytes 278528
  (19 other events, 50.7 us)
Sparse Core Ops, SparseCore 0:
  130.9 52.4 reduce-scatter.14
  213.6 48.2 reduce-scatter.12
  264.4 69.8 reduce-scatter.16
  338.0 207.6 reduce-scatter.20
  549.8 199.1 reduce-scatter.18
  752.6 194.2 reduce-scatter.22
where the time goes:
time: 960 us; the launch traced here: 956 us
  waiting for transfers between devices  754 us (79%)
  local copies, waits for them, and re-layouts  91.3 us (10%)
  matrix products  51.7 us (5%)
  between operations  21.4 us (2%)
  other arithmetic  20.9 us (2%)
  starting transfers between devices  16.6 us (2%)
    unnamed x9, waiting for transfers between devices  607 us
    reduce_scatter x1, waiting for transfers between devices, on_device(): lax.psum_scatter(merge_part.astype(jnp.bfloat16), 'lon', scatter_dimensio...  68.7 us
    reduce_scatter x1, waiting for transfers between devices, on_device(): lax.psum_scatter(qkv_part.astype(jnp.bfloat16), 'lon', scatter_dimension=...  39 us
    unnamed x68, local copies, waits for them, and re-layouts  26.9 us
    ppermute x4, waiting for transfers between devices, with_halo(): after = lax.ppermute(leading, axis, down)  23 us
  transfers between devices with their start and end apart: 14, of which 11 were waited for; matrix products, arithmetic and copies ran while one was open for 10% of the time, Pallas kernels for 0%

commit v1 on v0

--- a/solution.py
+++ b/solution.py
@@ -1,10 +1,279 @@
 import jax
 import jax.numpy as jnp
 from jax import lax
+from jax.experimental import pallas as pl
+from jax.experimental.pallas import tpu as pltpu
 from jax.sharding import PartitionSpec as P
 
 HEADS = 16
 WIN = 8
+
+
+XS, YLO, CORES, YHI, ZS = 4, 2, 2, 2, 8
+YS = YLO * YHI
+MESH = pl.DeviceIdType.MESH
+
+
+class Place:
+    def __init__(self):
+        lon = lax.axis_index("lon")
+        lat = lax.axis_index("lat")
+        self.lon, self.lat = lon, lat
+        self.core = lon % CORES
+        self.ylo = (lon // CORES) % YLO
+        self.x = lon // (CORES * YLO)
+        self.z = lat % ZS
+        self.yhi = lat // ZS
+
+    def at(self, x=None, ylo=None, core=None, yhi=None, z=None):
+        x = self.x if x is None else x
+        ylo = self.ylo if ylo is None else ylo
+        core = self.core if core is None else core
+        yhi = self.yhi if yhi is None else yhi
+        z = self.z if z is None else z
+        return ((x * YLO + ylo) * CORES + core, yhi * ZS + z)
+
+    def sibling(self):
+        return self.at(core=1 - self.core)
+
+    def x_step(self, k):
+        return (self.x + k) % XS
+
+    def y_step(self, k):
+        y = (self.yhi * YLO + self.ylo + k) % YS
+        return (y // YLO, y % YLO)
+
+    def z_step(self, k):
+        return (self.z + k) % ZS
+
+    def sum_partners(self):
+        out = [self.sibling()]
+        out += [self.at(x=self.x_step(k)) for k in range(1, XS)]
+        for k in range(1, YS):
+            yhi, ylo = self.y_step(k)
+            out.append(self.at(yhi=yhi, ylo=ylo))
+        out += [self.at(z=self.z_step(k)) for k in range(1, ZS)]
+        return out
+
+
+def device_of(pair):
+    return {"lon": pair[0], "lat": pair[1]}
+
+
+def greet(partners):
+    barrier = pltpu.get_barrier_semaphore()
+    for pair in partners:
+        pl.semaphore_signal(barrier, inc=1, device_id=device_of(pair), device_id_type=MESH)
+    pl.semaphore_wait(barrier, len(partners))
+
+
+HALF = ZS // 2
+
+
+def sum_scratch(rows):
+    b16 = jnp.bfloat16
+    copies = 2 + 2 * ((XS - 1) + (YS - 1)) + (ZS - 1)
+    return [
+        pltpu.VMEM((XS, YLO, YHI, ZS, rows, 128), b16),
+        pltpu.VMEM((XS - 1, YLO, YHI, HALF, rows, 128), b16),
+        pltpu.VMEM((YS - 1, XS, HALF, rows, 128), b16),
+        pltpu.VMEM((YLO, YHI, HALF, rows, 128), b16),
+        pltpu.VMEM((XS, HALF, rows, 128), b16),
+        pltpu.VMEM((YS - 1, HALF, rows, 128), b16),
+        pltpu.VMEM((XS - 1, HALF, rows, 128), b16),
+        pltpu.VMEM((ZS, rows, 128), b16),
+        pltpu.VMEM((ZS - 1, rows, 128), b16),
+        pltpu.SemaphoreType.DMA((copies,)),
+        pltpu.SemaphoreType.DMA((copies,)),
+    ]
+
+
+class Summing:
+    def __init__(self, place, parts, scratch):
+        (self.kept, self.from_x, self.from_y, self.sum_x, self.sum_y) = scratch[:5]
+        (self.late_y, self.late_x, self.column, self.from_z) = scratch[5:9]
+        self.send, self.recv = scratch[9:]
+        self.parts, self.place = parts, place
+        self.used = 0
+        self.flying = {}
+
+    def copy(self, src, dst, pair):
+        slot = self.used
+        self.used += 1
+        made = pltpu.make_async_remote_copy(
+            src_ref=src,
+            dst_ref=dst,
+            send_sem=self.send.at[slot],
+            recv_sem=self.recv.at[slot],
+            device_id=device_of(pair),
+            device_id_type=MESH,
+        )
+        made.start()
+        return made
+
+    def start_core(self):
+        other = 1 - self.place.core
+        self.flying["core"] = [
+            self.copy(
+                self.parts.at[:, :, other, :, pl.ds(h * HALF, HALF)],
+                self.kept.at[:, :, :, pl.ds(h * HALF, HALF)],
+                self.place.sibling(),
+            )
+            for h in range(2)
+        ]
+
+    def add_core(self, h):
+        core = self.place.core
+        self.flying["core"][h].wait()
+
+        def body(i, carry):
+            x, rest = i // (YLO * YHI), i % (YLO * YHI)
+            ylo, yhi = rest // YHI, rest % YHI
+            zs = pl.ds(h * HALF, HALF)
+            own = self.parts[x, ylo, core, yhi, zs].astype(jnp.float32)
+            got = self.kept[x, ylo, yhi, zs].astype(jnp.float32)
+            self.kept[x, ylo, yhi, zs] = (own + got).astype(jnp.bfloat16)
+            return carry
+
+        lax.fori_loop(0, XS * YLO * YHI, body, 0)
+
+    def start_first(self, h):
+        place = self.place
+        zs = pl.ds(h * HALF, HALF)
+        if h == 0:
+            self.flying["x"] = [
+                self.copy(
+                    self.kept.at[place.x_step(k), :, :, zs],
+                    self.from_x.at[k - 1],
+                    place.at(x=place.x_step(k)),
+                )
+                for k in range(1, XS)
+            ]
+        else:
+            self.flying["y"] = []
+            for k in range(1, YS):
+                yhi, ylo = place.y_step(k)
+                self.flying["y"].append(
+                    self.copy(
+                        self.kept.at[:, ylo, yhi, zs],
+                        self.from_y.at[k - 1],
+                        place.at(yhi=yhi, ylo=ylo),
+                    )
+                )
+
+    def add_first(self, h):
+        place = self.place
+        zs = pl.ds(h * HALF, HALF)
+        for made in self.flying["x" if h == 0 else "y"]:
+            made.wait()
+        if h == 0:
+
+            def body(i, carry):
+                ylo, yhi = i // YHI, i % YHI
+                total = self.kept[place.x, ylo, yhi, zs].astype(jnp.float32)
+                for k in range(XS - 1):
+                    total += self.from_x[k, ylo, yhi].astype(jnp.float32)
+                self.sum_x[ylo, yhi] = total.astype(jnp.bfloat16)
+                return carry
+
+            lax.fori_loop(0, YLO * YHI, body, 0)
+        else:
+
+            def body(x, carry):
+                total = self.kept[x, place.ylo, place.yhi, zs].astype(jnp.float32)
+                for k in range(YS - 1):
+                    total += self.from_y[k, x].astype(jnp.float32)
+                self.sum_y[x] = total.astype(jnp.bfloat16)
+                return carry
+
+            lax.fori_loop(0, XS, body, 0)
+
+    def start_second(self, h):
+        place = self.place
+        if h == 0:
+            self.flying["late_y"] = []
+            for k in range(1, YS):
+                yhi, ylo = place.y_step(k)
+                self.flying["late_y"].append(
+                    self.copy(
+                        self.sum_x.at[ylo, yhi],
+                        self.late_y.at[k - 1],
+                        place.at(yhi=yhi, ylo=ylo),
+                    )
+                )
+        else:
+            self.flying["late_x"] = [
+                self.copy(
+                    self.sum_y.at[place.x_step(k)],
+                    self.late_x.at[k - 1],
+                    place.at(x=place.x_step(k)),
+                )
+                for k in range(1, XS)
+            ]
+
+    def add_second(self, h):
+        place = self.place
+        for made in self.flying["late_y" if h == 0 else "late_x"]:
+            made.wait()
+        if h == 0:
+            total = self.sum_x[place.ylo, place.yhi].astype(jnp.float32)
+            for k in range(YS - 1):
+                total += self.late_y[k].astype(jnp.float32)
+        else:
+            total = self.sum_y[place.x].astype(jnp.float32)
+            for k in range(XS - 1):
+                total += self.late_x[k].astype(jnp.float32)
+        self.column[pl.ds(h * HALF, HALF)] = total.astype(jnp.bfloat16)
+
+    def start_last(self):
+        place = self.place
+        self.flying["z"] = [
+            self.copy(
+                self.column.at[place.z_step(k)],
+                self.from_z.at[k - 1],
+                place.at(z=place.z_step(k)),
+            )
+            for k in range(1, ZS)
+        ]
+
+    def add_last(self, out):
+        for made in self.flying["z"]:
+            made.wait()
+        total = self.column[self.place.z].astype(jnp.float32)
+        for k in range(ZS - 1):
+            total += self.from_z[k].astype(jnp.float32)
+        out[...] = total
+
+
+def sum_kernel(parts, out, *scratch):
+    place = Place()
+    greet(place.sum_partners())
+    work = Summing(place, parts, scratch)
+    work.start_core()
+    for h in range(2):
+        work.add_core(h)
+        work.start_first(h)
+    for h in range(2):
+        work.add_first(h)
+        work.start_second(h)
+    for h in range(2):
+        work.add_second(h)
+    work.start_last()
+    work.add_last(out)
+
+
+def weight_sums(parts):
+    rows = parts.shape[5]
+    return pl.pallas_call(
+        sum_kernel,
+        out_shape=jax.ShapeDtypeStruct((rows, 128), jnp.float32),
+        in_specs=[pl.BlockSpec(memory_space=pltpu.VMEM)],
+        out_specs=pl.BlockSpec(memory_space=pltpu.VMEM),
+        scratch_shapes=sum_scratch(rows),
+        compiler_params=pltpu.CompilerParams(
+            collective_id=0, has_side_effects=True, vmem_limit_bytes=48 * 2**20
+        ),
+    )(parts)
 
 
 EPSILON = 1e-05
@@ -219,29 +488,23 @@
     input_grad = (total_grad.astype(jnp.float32) + norm_back(hidden_grad, normed, inverse)).astype(
         jnp.bfloat16
     )
-    sectioned = (
-        lax.psum_scatter(
-            qkv_part.astype(jnp.bfloat16), "lon", scatter_dimension=0, tiled=True
-        ).astype(jnp.float32),
-        lax.psum_scatter(
-            proj_part.astype(jnp.bfloat16), "lon", scatter_dimension=0, tiled=True
-        ).astype(jnp.float32),
-        lax.psum_scatter(
-            merge_part.astype(jnp.bfloat16), "lon", scatter_dimension=0, tiled=True
-        ).astype(jnp.float32),
-    )
-    reduced = (
-        lax.psum_scatter(
-            sectioned[0].astype(jnp.bfloat16), "lat", scatter_dimension=1, tiled=True
-        ).astype(jnp.float32),
-        lax.psum_scatter(
-            sectioned[1].astype(jnp.bfloat16), "lat", scatter_dimension=1, tiled=True
-        ).astype(jnp.float32),
-        lax.psum_scatter(
-            sectioned[2].astype(jnp.bfloat16), "lat", scatter_dimension=1, tiled=True
-        ).astype(jnp.float32),
-    )
-    return (skip_out, merged_out, input_grad, reduced[0], reduced[1], reduced[2])
+    merge_block = (
+        merge_part.astype(jnp.bfloat16)
+        .reshape(XS, YLO, CORES, 128, YHI, ZS, 64)
+        .transpose(0, 1, 2, 4, 5, 6, 3)
+    )
+    qkv_block = qkv_part.astype(jnp.bfloat16).reshape(XS, YLO, CORES, 32, YHI, ZS, 96)
+    proj_block = proj_part.astype(jnp.bfloat16).reshape(XS, YLO, CORES, 32, YHI, ZS, 32)
+    fine_block = jnp.concatenate([qkv_block, proj_block], axis=-1).transpose(0, 1, 2, 4, 5, 3, 6)
+    mine = weight_sums(jnp.concatenate([merge_block, fine_block], axis=5))
+    return (
+        skip_out,
+        merged_out,
+        input_grad,
+        mine[64:, :96],
+        mine[64:, 96:],
+        mine[:64].T,
+    )
 
 
 def solution(mesh):

time: 960 us -> 297 us (0.31)
  waiting for transfers between devices: 754 us -> 23.1 us
  Pallas kernels: 0 us -> 47.3 us
  local copies, waits for them, and re-layouts: 91.3 us -> 122 us
  between operations: 21.4 us -> 8.16 us
    unnamed x9 -> x0, waiting for transfers between devices: 607 us -> none
    reduce_scatter x3 -> x0, waiting for transfers between devices: 108 us -> none  [the longest x1 68.7 us: on_device(): lax.psum_scatter(merge_part.astype(jnp.bfloat16), 'lon', scatter_dimensio...]
    pallas_call x0 -> x1, Pallas kernels: none -> 47.3 us  [weight_sums(): pl.pallas_call(sum_kernel, out_shape=jax.ShapeDtypeStruct((rows, 128), jn...]
    reshape x0 -> x6, local copies, waits for them, and re-layouts: none -> 35.7 us  [the longest x2 21.9 us: on_device(): merge_block = merge_part.astype(jnp.bfloat16).reshape(XS, YLO, CORES, 128...]
    ppermute x4, waiting for transfers between devices: 23 us -> 3.24 us  [with_halo(): after = lax.ppermute(leading, axis, down)]
    unnamed x68 -> x61, local copies, waits for them, and re-layouts: 26.9 us -> 19.9 us
  transfers between devices with their start and end apart: 14 -> 8, of which waited for: 11 -> 4; matrix products, arithmetic and copies ran while one was open for 10% -> 14% of each run, Pallas kernels for 0% -> 0%
where the time goes in v1:
time: 297 us; the launch traced here: 292 us
  local copies, waits for them, and re-layouts  122 us (41%)
  matrix products  49.8 us (17%)
  Pallas kernels  47.3 us (16%)
  other arithmetic  25.7 us (9%)
  waiting for transfers between devices  23.1 us (8%)
  starting transfers between devices  16.5 us (6%)
  between operations  8.16 us (3%)
    pallas_call x1, Pallas kernels, weight_sums(): pl.pallas_call(sum_kernel, out_shape=jax.ShapeDtypeStruct((rows, 128), jn...  47.3 us
    reshape x2, local copies, waits for them, and re-layouts, on_device(): merge_block = merge_part.astype(jnp.bfloat16).reshape(XS, YLO, CORES, 128...  21.9 us
    unnamed x61, local copies, waits for them, and re-layouts  19.9 us
    ppermute x4, waiting for transfers between devices, with_halo(): before = lax.ppermute(last, axis, up)  19.9 us
    concatenate x3, local copies, waits for them, and re-layouts, attend_back(): jnp.concatenate([query_grad.reshape(windows, per_window, -1), key_grad.re...  14.1 us
    ppermute x4, starting transfers between devices, with_halo(): after = lax.ppermute(leading, axis, down)  14 us
    dot_general x1, matrix products, attend_back(): jnp.einsum('nhqk,nqhd->nkhd', score_grad, queries, preferred_element_type...  10.3 us
    dot_general x1, matrix products, attend_back(): jnp.einsum('nhqk,nkhd->nqhd', score_grad, key_rows, preferred_element_typ...  10.1 us
  transfers between devices with their start and end apart: 8, of which 4 were waited for; matrix products, arithmetic and copies ran while one was open for 14% of the time, Pallas kernels for 0%

profile of v1, /device:TPU:4, one launch (start us, length us, event | category | flops | bytes accessed | tf_op | source)
XLA Modules:
  0.0 292.0 jit_solution(3492838172103865213)
XLA Ops:
  14.1 6.9 %collective-permute-start.3 = (bf16[8,48,1536]{2,1,0:T(8,128)(2,1)S(1)}, bf16[8,48,1536]{2,1,0:T(8,128)(2,1)}, u32[]{:S(2)}, u32[]{:S(2)}) collective-permute-start(bf16[8,48,1536]{2,1,0:T(8,128)(2,1)S(1)} %pad_maximum_fusion.1), channel_id=1, source_target_pairs={{1,0},{2,1},{3,2},{4,3},{5,4},{6,5},{7,6},{8,7},{9,8},{10,9},{11,1... | collective-permute-start | bytes 3538952 | tf_op jit(solution)/shard_map/ppermute | solution.py:291
  30.7 16.1 %collective-permute-done.2 = bf16[8,48,1536]{2,1,0:T(8,128)(2,1)} collective-permute-done((bf16[8,48,1536]{2,1,0:T(8,128)(2,1)S(1)}, bf16[8,48,1536]{2,1,0:T(8,128)(2,1)}, u32[]{:S(2)}, u32[]{:S(2)}) %collective-permute-start.2) | collective-permute-done | bytes 1179680 | tf_op jit(solution)/shard_map/ppermute | solution.py:290
  46.8 5.6 %fusion.22 = bf16[16,40,1536]{2,1,0:T(8,128)(2,1)S(1)} fusion(s32[]{:T(128)S(6)} %select_n.31, s32[]{:T(128)S(6)} %select_n.32, bf16[8,48,1536]{2,1,0:T(8,128)(2,1)} %collective-permute-done.2, bf16[8,8,1536]{2,1,0:T(8,128)(2,1)} %copy-done.14, bf16[8,32,1536]{2,1,0:T(8,128)(2,1)S(1)} %bitcast.107, bf16[8,8,1536]{2,1,0:T(8,128)(2,1)} %copy-done.13, ...), kind=kLoop, calls=%fused_computation.32 | loop fusion | flops 10813440 | bytes 5505048 | tf_op jit(solution)/shard_map/jit(_where)/select_n | solution.py:428
  52.7 7.1 %reshape_reshape.7 = bf16[10,64,3,16,32]{4,3,2,1,0:T(8,128)(2,1)} reshape(bf16[2,5,8,8,1536]{4,3,2,1,0:T(8,128)(2,1)S(1)} %copy.43) | data formatting | bytes 3932160 | tf_op jit(solution)/shard_map/reshape;reshape | solution.py:356
  59.7 5.6 %fusion.84 = (bf16[10,64,1,16,32]{4,3,2,1,0:T(8,128)(2,1)}, bf16[10,64,1,16,32]{4,3,2,1,0:T(8,128)(2,1)}, bf16[10,64,1,16,32]{4,3,2,1,0:T(8,128)(2,1)}) fusion(bf16[10,64,3,16,32]{4,3,2,1,0:T(8,128)(2,1)} %reshape_reshape.7), kind=kLoop, calls=%fused_computation.123 | loop fusion | bytes 3932160 | tf_op jit(solution)/shard_map/slice | solution.py:357
  65.3 4.7 %copy.72 = bf16[10,64,1,16,32]{1,4,3,0,2:T(8,128)(2,1)} copy(bf16[10,64,1,16,32]{4,3,2,1,0:T(8,128)(2,1)} %get-tuple-element.11) | data formatting | bytes 1310720
  73.9 5.1 %copy.73 = bf16[10,64,1,16,32]{1,4,3,0,2:T(8,128)(2,1)} copy(bf16[10,64,1,16,32]{4,3,2,1,0:T(8,128)(2,1)} %get-tuple-element.10) | data formatting | bytes 1310720
  90.9 4.4 %convert_element_type.98 = bf16[2,5,8,8,512]{4,3,2,1,0:T(8,128)(2,1)S(1)} reshape(bf16[10,64,16,32]{3,2,1,0:T(8,128)(2,1)} %copy.48) | data formatting | bytes 1310720 | tf_op jit(solution)/shard_map/convert_element_type | solution.py:377
  115.5 6.0 %collective-permute-start.7 = (bf16[8,48,512]{2,1,0:T(8,128)(2,1)}, bf16[8,48,512]{2,1,0:T(8,128)(2,1)}, u32[]{:S(2)}, u32[]{:S(2)}) collective-permute-start(bf16[8,48,512]{2,1,0:T(8,128)(2,1)} %pad_maximum_fusion.2), channel_id=1, source_target_pairs={{1,0},{2,1},{3,2},{4,3},{5,4},{6,5},{7,6},{8,7},{9,8},{10,9},{11,1... | collective-permute-start | bytes 1179656 | tf_op jit(solution)/shard_map/ppermute | solution.py:291
  131.4 11.6 %reshape.190 = bf16[4,2,2,128,2,8,64]{6,5,4,3,2,1,0:T(8,128)(2,1)} reshape(bf16[2048,1024]{1,0:T(8,128)(2,1)} %bitcast_convert_fusion) | data formatting | bytes 8388608 | tf_op jit(solution)/shard_map/reshape | solution.py:493
  143.0 10.3 %copy.63 = bf16[4,2,2,128,2,8,64]{3,6,5,4,2,1,0:T(8,128)(2,1)} copy(bf16[4,2,2,128,2,8,64]{6,5,4,3,2,1,0:T(8,128)(2,1)} %reshape.190) | data formatting | bytes 8388608 | tf_op jit(solution)/shard_map/reshape | solution.py:493
  162.4 4.9 %copy.53 = bf16[10,64,16,32]{1,3,2,0:T(8,128)(2,1)} copy(bf16[10,64,16,32]{3,2,1,0:T(8,128)(2,1)} %reshape_reshape.8) | data formatting | bytes 1310720 | tf_op jit(solution)/shard_map/reshape;reshape | solution.py:386
  167.3 5.6 %convolution_bitcast_fusion.1 = bf16[10,64,16,32]{1,3,2,0:T(8,128)(2,1)} fusion(bf16[10,64,16,32]{1,3,2,0:T(8,128)(2,1)} %copy.53, f32[10,16,64,64]{2,3,1,0:T(8,128)} %copy-done.26, f32[10,16,64]{2,1,0:T(8,128)S(1)} %copy-done.28), kind=kOutput, calls=%fused_computation.35 | convolution fusion | flops 43253760 | bytes 3973120 | tf_op jit(solution)/shard_map/nhqk,nqhd->nkhd/dot_general | solution.py:398
  176.1 10.3 %fusion.28 = bf16[10,64,16,32]{1,3,2,0:T(8,128)(2,1)} fusion(f32[10,16,64,64]{2,3,1,0:T(8,128)} %fusion.39, bf16[10,64,1,16,32]{1,4,3,0,2:T(8,128)(2,1)} %copy.73, f32[10,16,64,64]{2,3,1,0:T(8,128)} %copy-done.26, f32[10,16,64]{2,1,0:T(8,128)S(1)} %copy-done.28), kind=kOutput, calls=%fused_computation.37 | convolution fusion | flops 46540864 | bytes 6594560 | tf_op jit(solution)/shard_map/nhqk,nqhd->nkhd/dot_general | solution.py:395
  186.3 10.1 %fusion.25 = bf16[10,64,16,32]{1,3,2,0:T(8,128)(2,1)} fusion(f32[10,16,64,64]{2,3,1,0:T(8,128)} %fusion.39, bf16[10,64,1,16,32]{1,4,3,0,2:T(8,128)(2,1)} %copy-done.4, f32[10,16,64,64]{2,3,1,0:T(8,128)} %copy-done.26, f32[10,16,64]{2,1,0:T(8,128)S(1)} %copy-done.28), kind=kOutput, calls=%fused_computation.36 | convolution fusion | flops 46540864 | bytes 6594560 | tf_op jit(solution)/shard_map/nhqk,nkhd->nqhd/dot_general | solution.py:392
  196.5 4.4 %copy.60 = bf16[10,64,16,32]{3,2,1,0:T(8,128)(2,1)} copy(bf16[10,64,16,32]{1,3,2,0:T(8,128)(2,1)} %convolution_bitcast_fusion.1) | data formatting | bytes 1310720 | tf_op jit(solution)/shard_map/nhqk,nqhd->nkhd/transpose | solution.py:398
  200.9 4.1 %concatenate.34 = bf16[2,5,8,8,512]{4,3,2,1,0:T(8,128)(2,1)S(1)} reshape(bf16[10,64,16,32]{3,2,1,0:T(8,128)(2,1)} %copy.60) | data formatting | bytes 1310720 | tf_op jit(solution)/shard_map/concatenate | solution.py:401
  205.1 4.5 %copy.57 = bf16[10,64,16,32]{3,2,1,0:T(8,128)(2,1)} copy(bf16[10,64,16,32]{1,3,2,0:T(8,128)(2,1)} %fusion.28) | data formatting | bytes 1310720 | tf_op jit(solution)/shard_map/nhqk,nqhd->nkhd/transpose | solution.py:395
  209.5 4.8 %concatenate.33 = bf16[2,5,8,8,512]{4,3,2,1,0:T(8,128)(2,1)} reshape(bf16[10,64,16,32]{3,2,1,0:T(8,128)(2,1)} %copy.57) | data formatting | bytes 1310720 | tf_op jit(solution)/shard_map/concatenate | solution.py:401
  214.4 4.4 %copy.55 = bf16[10,64,16,32]{3,2,1,0:T(8,128)(2,1)} copy(bf16[10,64,16,32]{1,3,2,0:T(8,128)(2,1)} %fusion.25) | data formatting | bytes 1310720 | tf_op jit(solution)/shard_map/nhqk,nkhd->nqhd/transpose | solution.py:392
  218.8 5.1 %concatenate.32 = bf16[2,5,8,8,512]{4,3,2,1,0:T(8,128)(2,1)} reshape(bf16[10,64,16,32]{3,2,1,0:T(8,128)(2,1)} %copy.55) | data formatting | bytes 1310720 | tf_op jit(solution)/shard_map/concatenate | solution.py:401
  228.5 4.3 %reshape.177 = bf16[4,2,2,32,2,8,96]{6,5,4,3,2,1,0:T(8,128)(2,1)} reshape(bf16[512,1536]{1,0:T(8,128)(2,1)} %fusion.8) | data formatting | bytes 3145728 | tf_op jit(solution)/shard_map/reshape | solution.py:496
  237.4 4.0 %pad_maximum_fusion.parts = bf16[4,2,2,2,8,96,128]{6,5,4,3,2,1,0:T(8,128)(2,1)} fusion(bf16[4,2,2,2,8,32,128]{6,5,4,3,2,1,0:T(8,128)(2,1)S(1)} %maximum_bitcast_fusion.1, bf16[4,2,2,2,8,64,128]{6,5,4,3,2,1,0:T(8,128)(2,1)S(1)} %bitcast.104), kind=kLoop, calls=%fused_computation.3 | loop fusion | flops 12582912 | bytes 12582912 | tf_op jit(solution)/shard_map/concatenate | solution.py:499
  241.3 47.3 %shard_map.118 = f32[96,128]{1,0:T(8,128)S(1)} custom-call(bf16[4,2,2,2,8,96,128]{6,5,4,3,2,1,0:T(8,128)(2,1)} %pad_maximum_fusion.parts), custom_call_target="tpu_custom_call" | custom-call | tf_op jit(solution)/shard_map/pallas_call | solution.py:267
  (134 shorter events, 86.7 us)
Async XLA Ops:
  4.1 4.9 %copy-start.10 = (bf16[8,32,512]{2,1,0:T(8,128)(2,1)}, bf16[8,32,512]{2,1,0:T(8,128)(2,1)S(1)}, u32[]{:S(2)}) copy-start(bf16[8,32,512]{2,1,0:T(8,128)(2,1)S(1)} %fusion.55) | copy-start | bytes 786436
  4.2 16.8 %copy-start.22 = (s32[2]{0:T(128)S(1)}, s32[2]{0:T(128)}, u32[]{:S(2)}) copy-start(s32[2]{0:T(128)} %param.13) | copy-start | bytes 28
  4.8 4.3 %collective-permute-start.1 = (bf16[8,8,1536]{2,1,0:T(8,128)(2,1)S(1)}, bf16[8,8,1536]{2,1,0:T(8,128)(2,1)S(1)}, u32[]{:S(2)}, u32[]{:S(2)}) collective-permute-start(bf16[8,8,1536]{2,1,0:T(8,128)(2,1)S(1)} %get-tuple-element.14), channel_id=1, source_target_pairs={{16,0},{32,16},{48,32},{64,48},{80,64},{96,80},{112,96},{128,112},... | collective-permute-start | bytes 589832 | tf_op jit(solution)/shard_map/ppermute | solution.py:291
  5.9 6.1 %collective-permute-start = (bf16[8,8,1536]{2,1,0:T(8,128)(2,1)S(1)}, bf16[8,8,1536]{2,1,0:T(8,128)(2,1)S(1)}, u32[]{:S(2)}, u32[]{:S(2)}) collective-permute-start(bf16[8,8,1536]{2,1,0:T(8,128)(2,1)S(1)} %get-tuple-element.13), channel_id=1, source_target_pairs={{0,16},{16,32},{32,48},{48,64},{64,80},{80,96},{96,112},{112,128},... | collective-permute-start | bytes 589832 | tf_op jit(solution)/shard_map/ppermute | solution.py:290
  9.1 11.9 %copy-start.13 = (bf16[8,8,1536]{2,1,0:T(8,128)(2,1)}, bf16[8,8,1536]{2,1,0:T(8,128)(2,1)S(1)}, u32[]{:S(2)}) copy-start(bf16[8,8,1536]{2,1,0:T(8,128)(2,1)S(1)} %collective-permute-done.1) | copy-start | bytes 589828
  12.0 9.0 %copy-start.14 = (bf16[8,8,1536]{2,1,0:T(8,128)(2,1)}, bf16[8,8,1536]{2,1,0:T(8,128)(2,1)S(1)}, u32[]{:S(2)}) copy-start(bf16[8,8,1536]{2,1,0:T(8,128)(2,1)S(1)} %collective-permute-done) | copy-start | bytes 589828
  12.1 34.8 %collective-permute-start.2 = (bf16[8,48,1536]{2,1,0:T(8,128)(2,1)S(1)}, bf16[8,48,1536]{2,1,0:T(8,128)(2,1)}, u32[]{:S(2)}, u32[]{:S(2)}) collective-permute-start(bf16[8,48,1536]{2,1,0:T(8,128)(2,1)S(1)} %pad_maximum_fusion.1), channel_id=1, source_target_pairs={{0,1},{1,2},{2,3},{3,4},{4,5},{5,6},{6,7},{7,8},{8,9},{9,10},{10,1... | collective-permute-start | bytes 3538952 | tf_op jit(solution)/shard_map/ppermute | solution.py:290
  14.1 32.8 %collective-permute-start.3 = (bf16[8,48,1536]{2,1,0:T(8,128)(2,1)S(1)}, bf16[8,48,1536]{2,1,0:T(8,128)(2,1)}, u32[]{:S(2)}, u32[]{:S(2)}) collective-permute-start(bf16[8,48,1536]{2,1,0:T(8,128)(2,1)S(1)} %pad_maximum_fusion.1), channel_id=1, source_target_pairs={{1,0},{2,1},{3,2},{4,3},{5,4},{6,5},{7,6},{8,7},{9,8},{10,9},{11,1... | collective-permute-start | bytes 3538952 | tf_op jit(solution)/shard_map/ppermute | solution.py:291
  73.9 7.4 %copy-start.4 = (bf16[10,64,1,16,32]{1,4,3,0,2:T(8,128)(2,1)}, bf16[10,64,1,16,32]{1,4,3,0,2:T(8,128)(2,1)S(1)}, u32[]{:S(2)}) copy-start(bf16[10,64,1,16,32]{1,4,3,0,2:T(8,128)(2,1)S(1)} %copy.74) | copy-start | bytes 1966084
  81.3 5.3 %copy-start.5 = (bf16[10,64,1,16,32]{1,4,3,0,2:T(8,128)(2,1)S(1)}, bf16[10,64,1,16,32]{1,4,3,0,2:T(8,128)(2,1)}, u32[]{:S(2)}) copy-start(bf16[10,64,1,16,32]{1,4,3,0,2:T(8,128)(2,1)} %copy.72) | copy-start | bytes 1966084
  90.9 5.3 %copy-start.3 = (bf16[8,32,512]{2,1,0:T(8,128)(2,1)S(1)}, bf16[8,32,512]{2,1,0:T(8,128)(2,1)}, u32[]{:S(2)}) copy-start(bf16[8,32,512]{2,1,0:T(8,128)(2,1)} %param.7) | copy-start | bytes 786436
  90.9 5.3 %copy-start.8 = (bf16[512,512]{1,0:T(8,128)(2,1)S(1)}, bf16[512,512]{1,0:T(8,128)(2,1)}, u32[]{:S(2)}) copy-start(bf16[512,512]{1,0:T(8,128)(2,1)} %param.9) | copy-start | bytes 1572868
  110.0 3.9 %collective-permute-start.5 = (bf16[8,8,512]{2,1,0:T(8,128)(2,1)S(1)}, bf16[8,8,512]{2,1,0:T(8,128)(2,1)S(1)}, u32[]{:S(2)}, u32[]{:S(2)}) collective-permute-start(bf16[8,8,512]{2,1,0:T(8,128)(2,1)S(1)} %get-tuple-element.16), channel_id=1, source_target_pairs={{16,0},{32,16},{48,32},{64,48},{80,64},{96,80},{112,96},{128,112},... | collective-permute-start | bytes 196616 | tf_op jit(solution)/shard_map/ppermute | solution.py:291
  110.1 4.7 %collective-permute-start.4 = (bf16[8,8,512]{2,1,0:T(8,128)(2,1)S(1)}, bf16[8,8,512]{2,1,0:T(8,128)(2,1)S(1)}, u32[]{:S(2)}, u32[]{:S(2)}) collective-permute-start(bf16[8,8,512]{2,1,0:T(8,128)(2,1)S(1)} %get-tuple-element.15), channel_id=1, source_target_pairs={{0,16},{16,32},{32,48},{48,64},{64,80},{80,96},{96,112},{112,128},... | collective-permute-start | bytes 196616 | tf_op jit(solution)/shard_map/ppermute | solution.py:290
  113.8 7.6 %copy-start.16 = (bf16[8,8,512]{2,1,0:T(8,128)(2,1)}, bf16[8,8,512]{2,1,0:T(8,128)(2,1)S(1)}, u32[]{:S(2)}) copy-start(bf16[8,8,512]{2,1,0:T(8,128)(2,1)S(1)} %collective-permute-done.5) | copy-start | bytes 196612
  114.7 6.8 %copy-start.18 = (bf16[8,8,512]{2,1,0:T(8,128)(2,1)}, bf16[8,8,512]{2,1,0:T(8,128)(2,1)S(1)}, u32[]{:S(2)}) copy-start(bf16[8,8,512]{2,1,0:T(8,128)(2,1)S(1)} %collective-permute-done.4) | copy-start | bytes 196612
  115.5 41.6 %collective-permute-start.6 = (bf16[8,48,512]{2,1,0:T(8,128)(2,1)}, bf16[8,48,512]{2,1,0:T(8,128)(2,1)}, u32[]{:S(2)}, u32[]{:S(2)}) collective-permute-start(bf16[8,48,512]{2,1,0:T(8,128)(2,1)} %pad_maximum_fusion.2), channel_id=1, source_target_pairs={{0,1},{1,2},{2,3},{3,4},{4,5},{5,6},{6,7},{7,8},{8,9},{9,10},{10,1... | collective-permute-start | bytes 1179656 | tf_op jit(solution)/shard_map/ppermute | solution.py:290
  115.5 41.6 %collective-permute-start.7 = (bf16[8,48,512]{2,1,0:T(8,128)(2,1)}, bf16[8,48,512]{2,1,0:T(8,128)(2,1)}, u32[]{:S(2)}, u32[]{:S(2)}) collective-permute-start(bf16[8,48,512]{2,1,0:T(8,128)(2,1)} %pad_maximum_fusion.2), channel_id=1, source_target_pairs={{1,0},{2,1},{3,2},{4,3},{5,4},{6,5},{7,6},{8,7},{9,8},{10,9},{11,1... | collective-permute-start | bytes 1179656 | tf_op jit(solution)/shard_map/ppermute | solution.py:291
  153.3 3.8 %copy-start.17 = (bf16[8,8,512]{2,1,0:T(8,128)(2,1)S(1)}, bf16[8,8,512]{2,1,0:T(8,128)(2,1)}, u32[]{:S(2)}) copy-start(bf16[8,8,512]{2,1,0:T(8,128)(2,1)} %copy-done.16) | copy-start | bytes 196612
  153.3 3.8 %copy-start.19 = (bf16[8,8,512]{2,1,0:T(8,128)(2,1)S(1)}, bf16[8,8,512]{2,1,0:T(8,128)(2,1)}, u32[]{:S(2)}) copy-start(bf16[8,8,512]{2,1,0:T(8,128)(2,1)} %copy-done.18) | copy-start | bytes 196612
  153.3 3.8 %copy-start.25 = (pred[16]{0:T(512)(128)(4,1)S(1)}, pred[16]{0:T(512)(128)(4,1)}, u32[]{:S(2)}) copy-start(pred[16]{0:T(512)(128)(4,1)} %copy-done.24) | copy-start | bytes 52
  162.4 4.9 %copy-start.28 = (f32[10,16,64]{2,1,0:T(8,128)S(1)}, f32[10,16,64]{2,1,0:T(8,128)}, u32[]{:S(2)}) copy-start(f32[10,16,64]{2,1,0:T(8,128)} %copy-done.27) | copy-start | bytes 122884
  167.3 5.6 %copy-start.6 = (bf16[10,64,1,16,32]{1,4,3,0,2:T(8,128)(2,1)S(1)}, bf16[10,64,1,16,32]{1,4,3,0,2:T(8,128)(2,1)}, u32[]{:S(2)}) copy-start(bf16[10,64,1,16,32]{1,4,3,0,2:T(8,128)(2,1)} %copy.72) | copy-start | bytes 1966084
  167.3 5.6 %copy-start.7 = (bf16[10,64,16,32]{1,3,2,0:T(8,128)(2,1)S(1)}, bf16[10,64,16,32]{1,3,2,0:T(8,128)(2,1)}, u32[]{:S(2)}) copy-start(bf16[10,64,16,32]{1,3,2,0:T(8,128)(2,1)} %copy.53) | copy-start | bytes 1966084
  (13 other events, 24.5 us)

commit v2 on v1

v2 whole, which is shorter than its diff:
```python
import jax
import jax.numpy as jnp
from jax import lax
from jax.experimental import pallas as pl
from jax.experimental.pallas import tpu as pltpu
from jax.sharding import PartitionSpec as P

HEADS = 16
WIN = 8
EPSILON = 1e-05
NEGATIVE = -1e30
D = 512
D2 = 1024
ROWS, COLS = 8, 32
CELLS = ROWS * COLS
ACROSS = COLS // WIN + 1
BAND = ACROSS * WIN * WIN
LAT = 128
FACTOR = 32 ** (-0.5)
MERGED = CELLS // 4
EDGE = ROWS * WIN
LEFT = 3 * CELLS
RIGHT = LEFT + 3 * EDGE
SOURCES = RIGHT + 3 * EDGE
F32, B16 = jnp.float32, jnp.bfloat16

XS, YLO, CORES, YHI, ZS = 4, 2, 2, 2, 8
YS = YLO * YHI
MESH = pl.DeviceIdType.MESH


class Place:
    def __init__(self):
        lon = lax.axis_index("lon")
        lat = lax.axis_index("lat")
        self.lon, self.lat = lon, lat
        self.core = lon % CORES
        self.ylo = (lon // CORES) % YLO
        self.x = lon // (CORES * YLO)
        self.z = lat % ZS
        self.yhi = lat // ZS

    def at(self, x=None, ylo=None, core=None, yhi=None, z=None):
        x = self.x if x is None else x
        ylo = self.ylo if ylo is None else ylo
        core = self.core if core is None else core
        yhi = self.yhi if yhi is None else yhi
        z = self.z if z is None else z
        return ((x * YLO + ylo) * CORES + core, yhi * ZS + z)

    def beside(self, dlat, dlon):
        lons, lats = XS * YLO * CORES, YHI * ZS
        return ((self.lon + dlon) % lons, (self.lat + dlat) % lats)

    def sibling(self):
        return self.at(core=1 - self.core)

    def x_step(self, k):
        return (self.x + k) % XS

    def y_step(self, k):
        y = (self.yhi * YLO + self.ylo + k) % YS
        return (y // YLO, y % YLO)

    def z_step(self, k):
        return (self.z + k) % ZS

    def sum_partners(self):
        out = [self.sibling()]
        out += [self.at(x=self.x_step(k)) for k in range(1, XS)]
        for k in range(1, YS):
            yhi, ylo = self.y_step(k)
            out.append(self.at(yhi=yhi, ylo=ylo))
        out += [self.at(z=self.z_step(k)) for k in range(1, ZS)]
        return out


def device_of(pair):
    return {"lon": pair[0], "lat": pair[1]}


def greet(partners):
    barrier = pltpu.get_barrier_semaphore()
    for pair in partners:
        pl.semaphore_signal(barrier, inc=1, device_id=device_of(pair), device_id_type=MESH)
    pl.semaphore_wait(barrier, len(partners))


HALF = ZS // 2


def sum_scratch(rows):
    b16 = jnp.bfloat16
    copies = 2 + 2 * ((XS - 1) + (YS - 1)) + (ZS - 1)
    return [
        pltpu.VMEM((XS, YLO, YHI, ZS, rows, 128), b16),
        pltpu.VMEM((XS - 1, YLO, YHI, HALF, rows, 128), b16),
        pltpu.VMEM((YS - 1, XS, HALF, rows, 128), b16),
        pltpu.VMEM((YLO, YHI, HALF, rows, 128), b16),
        pltpu.VMEM((XS, HALF, rows, 128), b16),
        pltpu.VMEM((YS - 1, HALF, rows, 128), b16),
        pltpu.VMEM((XS - 1, HALF, rows, 128), b16),
        pltpu.VMEM((ZS, rows, 128), b16),
        pltpu.VMEM((ZS - 1, rows, 128), b16),
        pltpu.SemaphoreType.DMA((copies,)),
        pltpu.SemaphoreType.DMA((copies,)),
    ]


class Summing:
    def __init__(self, place, parts, scratch):
        (self.kept, self.from_x, self.from_y, self.sum_x, self.sum_y) = scratch[:5]
        (self.late_y, self.late_x, self.column, self.from_z) = scratch[5:9]
        self.send, self.recv = scratch[9:]
        self.parts, self.place = parts, place
        self.used = 0
        self.flying = {}

    def copy(self, src, dst, pair):
        slot = self.used
        self.used += 1
        made = pltpu.make_async_remote_copy(
            src_ref=src,
            dst_ref=dst,
            send_sem=self.send.at[slot],
            recv_sem=self.recv.at[slot],
            device_id=device_of(pair),
            device_id_type=MESH,
        )
        made.start()
        return made

    def start_core(self):
        other = 1 - self.place.core
        self.flying["core"] = [
            self.copy(
                self.parts.at[:, :, other, :, pl.ds(h * HALF, HALF)],
                self.kept.at[:, :, :, pl.ds(h * HALF, HALF)],
                self.place.sibling(),
            )
            for h in range(2)
        ]

    def add_core(self, h):
        core = self.place.core
        self.flying["core"][h].wait()

        def body(i, carry):
            x, rest = i // (YLO * YHI), i % (YLO * YHI)
            ylo, yhi = rest // YHI, rest % YHI
            zs = pl.ds(h * HALF, HALF)
            own = self.parts[x, ylo, core, yhi, zs].astype(jnp.float32)
            got = self.kept[x, ylo, yhi, zs].astype(jnp.float32)
            self.kept[x, ylo, yhi, zs] = (own + got).astype(jnp.bfloat16)
            return carry

        lax.fori_loop(0, XS * YLO * YHI, body, 0)

    def start_first(self, h):
        place = self.place
        zs = pl.ds(h * HALF, HALF)
        if h == 0:
            self.flying["x"] = [
                self.copy(
                    self.kept.at[place.x_step(k), :, :, zs],
                    self.from_x.at[k - 1],
                    place.at(x=place.x_step(k)),
                )
                for k in range(1, XS)
            ]
        else:
            self.flying["y"] = []
            for k in range(1, YS):
                yhi, ylo = place.y_step(k)
                self.flying["y"].append(
                    self.copy(
                        self.kept.at[:, ylo, yhi, zs],
                        self.from_y.at[k - 1],
                        place.at(yhi=yhi, ylo=ylo),
                    )
                )

    def add_first(self, h):
        place = self.place
        zs = pl.ds(h * HALF, HALF)
        for made in self.flying["x" if h == 0 else "y"]:
            made.wait()
        if h == 0:

            def body(i, carry):
                ylo, yhi = i // YHI, i % YHI
                total = self.kept[place.x, ylo, yhi, zs].astype(jnp.float32)
                for k in range(XS - 1):
                    total += self.from_x[k, ylo, yhi].astype(jnp.float32)
                self.sum_x[ylo, yhi] = total.astype(jnp.bfloat16)
                return carry

            lax.fori_loop(0, YLO * YHI, body, 0)
        else:

            def body(x, carry):
                total = self.kept[x, place.ylo, place.yhi, zs].astype(jnp.float32)
                for k in range(YS - 1):
                    total += self.from_y[k, x].astype(jnp.float32)
                self.sum_y[x] = total.astype(jnp.bfloat16)
                return carry

            lax.fori_loop(0, XS, body, 0)

    def start_second(self, h):
        place = self.place
        if h == 0:
            self.flying["late_y"] = []
            for k in range(1, YS):
                yhi, ylo = place.y_step(k)
                self.flying["late_y"].append(
                    self.copy(
                        self.sum_x.at[ylo, yhi],
                        self.late_y.at[k - 1],
                        place.at(yhi=yhi, ylo=ylo),
                    )
                )
        else:
            self.flying["late_x"] = [
                self.copy(
                    self.sum_y.at[place.x_step(k)],
                    self.late_x.at[k - 1],
                    place.at(x=place.x_step(k)),
                )
                for k in range(1, XS)
            ]

    def add_second(self, h):
        place = self.place
        for made in self.flying["late_y" if h == 0 else "late_x"]:
            made.wait()
        if h == 0:
            total = self.sum_x[place.ylo, place.yhi].astype(jnp.float32)
            for k in range(YS - 1):
                total += self.late_y[k].astype(jnp.float32)
        else:
            total = self.sum_y[place.x].astype(jnp.float32)
            for k in range(XS - 1):
                total += self.late_x[k].astype(jnp.float32)
        self.column[pl.ds(h * HALF, HALF)] = total.astype(jnp.bfloat16)

    def start_last(self):
        place = self.place
        self.flying["z"] = [
            self.copy(
                self.column.at[place.z_step(k)],
                self.from_z.at[k - 1],
                place.at(z=place.z_step(k)),
            )
            for k in range(1, ZS)
        ]

    def add_last(self, out):
        for made in self.flying["z"]:
            made.wait()
        total = self.column[self.place.z].astype(jnp.float32)
        for k in range(ZS - 1):
            total += self.from_z[k].astype(jnp.float32)
        out[...] = total


def iota(shape, dim):
    return lax.broadcasted_iota(jnp.int32, shape, dim)


def one_hot(rows, cols, index):
    place = index(iota((rows, 1), 0))
    return jnp.where(iota((rows, cols), 1) == place, 1.0, 0.0).astype(B16)


def dot(a, b):
    return jnp.dot(a, b, preferred_element_type=F32)


def dot_nt(a, b):
    return lax.dot_general(a, b, (((1,), (1,)), ((), ())), preferred_element_type=F32)


def dot_tn(a, b):
    return lax.dot_general(a, b, (((0,), (0,)), ((), ())), preferred_element_type=F32)


def merge_order(n):
    part, r, c = n >> 6, (n >> 4) & 3, n & 15
    return 2 * r + (part & 1), 2 * c + (part >> 1)


def merge_index(n):
    i, j = n >> 5, n & 31
    return (((j & 1) * 2 + (i & 1)) << 6) + ((i >> 1) << 4) + (j >> 1)


def to_merged_index(n):
    i, j = merge_order(n)
    return i * COLS + j


def edge_index(n):
    return ((n >> 3) & 7) * COLS + (n & 7) + (n >> 6) * (COLS - WIN)


def normalize(values):
    center = values - jnp.mean(values, axis=-1, keepdims=True)
    inverse = lax.rsqrt(jnp.mean(center * center, axis=-1, keepdims=True) + EPSILON)
    return center * inverse, inverse


class Halo:
    def __init__(self, place, ext, edges, send, recv):
        self.place, self.ext, self.edges = place, ext, edges
        self.send, self.recv = send, recv

    def start(self, own):
        self.flying = []
        jobs = [(own, 0, 1, 0), (own, 2 * CELLS, -1, 0)]
        first, last = self.edges.at[pl.ds(0, EDGE)], self.edges.at[pl.ds(EDGE, EDGE)]
        for step in range(3):
            dlat = 1 - step
            jobs.append((last, LEFT + step * EDGE, dlat, 1))
            jobs.append((first, RIGHT + step * EDGE, dlat, -1))
        for slot, (src, offset, dlat, dlon) in enumerate(jobs):
            made = pltpu.make_async_remote_copy(
                src_ref=src,
                dst_ref=self.ext.at[pl.ds(offset, src.shape[0])],
                send_sem=self.send.at[slot],
                recv_sem=self.recv.at[slot],
                device_id=device_of(self.place.beside(dlat, dlon)),
                device_id_type=MESH,
            )
            made.start()
            self.flying.append(made)

    def wait(self):
        for made in self.flying:
            made.wait()


def halo_partners(place):
    return [
        place.beside(dlat, dlon)
        for dlat in (-1, 0, 1)
        for dlon in (-1, 0, 1)
        if (dlat, dlon) != (0, 0)
    ]


def band_of(ext, k, gather):
    source = jnp.concatenate(
        [
            ext[pl.ds(CELLS * k, 2 * CELLS)],
            ext[pl.ds(LEFT + EDGE * k, 2 * EDGE)],
            ext[pl.ds(RIGHT + EDGE * k, 2 * EDGE)],
        ],
        axis=0,
    )
    return dot(gather[...], source)


def row_valid(place, shift_lat, k, n):
    row = ROWS * place.lat - WIN + shift_lat + WIN * k + ((n >> 3) & 7)
    return (row >= 0) & (row < LAT)


def section_kernel(
    shift,
    tokens,
    skip_grad,
    merged_grad,
    w_qkv_hbm,
    w_proj_hbm,
    w_merge_hbm,
    skip_out,
    merged_out,
    input_grad,
    sum_merge,
    sum_fine,
    w_qkv,
    w_proj,
    w_merge,
    load,
    ext,
    ext_back,
    edges,
    edges_back,
    grad_own,
    halo_send,
    halo_recv,
    halo_back_send,
    halo_back_recv,
    gather,
    scatter,
    hidden,
    packed,
    probs,
    attended,
    back_in,
    packed_grad,
    own_both,
    spread,
    merged_hidden,
    total_grad,
    parts_merge,
    parts_fine,
    *scratch,
):
    place = Place()
    a, b = shift[0], shift[1]
    loads = [
        pltpu.make_async_copy(src, dst, load.at[n])
        for n, (src, dst) in enumerate(
            ((w_qkv_hbm, w_qkv), (w_proj_hbm, w_proj), (w_merge_hbm, w_merge))
        )
    ]
    for made in loads:
        made.start()
    count = len(scratch) // 2
    merge_sum = Summing(place, parts_merge, scratch[:count])
    fine_sum = Summing(place, parts_fine, scratch[count:])

    pick_edges = one_hot(2 * EDGE, CELLS, edge_index)
    edges[...] = dot(pick_edges, tokens[...]).astype(B16)
    greet(place.sum_partners() + halo_partners(place))
    halo = Halo(place, ext, edges, halo_send, halo_recv)
    halo.start(tokens)
    ext[pl.ds(CELLS, CELLS)] = tokens[...]

    def gather_index(n):
        w, i, j = n >> 6, (n >> 3) & 7, n & 7
        row, col = a + i, b + WIN * w + j - WIN
        inside = row * COLS + col
        left = 2 * CELLS + row * WIN + col + WIN
        right = 2 * CELLS + 2 * EDGE + row * WIN + col - COLS
        return jnp.where(col < 0, left, jnp.where(col >= COLS, right, inside))

    gather[...] = one_hot(BAND, 2 * CELLS + 4 * EDGE, gather_index)

    def scatter_index(n):
        i, j = merge_order(n)
        row, col = ROWS + i - a, WIN + j - b
        return (row >> 3) * BAND + ((col >> 3) << 6) + ((row & 7) << 3) + (col & 7)

    scatter[...] = one_hot(CELLS, 2 * BAND, scatter_index)
    to_merged = one_hot(CELLS, CELLS, to_merged_index)
    to_rows = one_hot(CELLS, CELLS, merge_index)
    own_tokens = dot(to_merged, tokens[...])
    own_normed, own_inverse = normalize(own_tokens)
    own_both[pl.ds(0, CELLS)] = own_normed.astype(B16)
    own_skip = dot(to_merged, skip_grad[...])
    grads = merged_grad[...]
    loads[2].wait()
    merged_back = [
        dot_nt(grads, w_merge[pl.ds(D * part, D)]) for part in range(4)
    ]
    loads[0].wait()
    loads[1].wait()

    halo.wait()
    for k in range(2):
        rows = pl.ds(BAND * k, BAND)
        normed, _ = normalize(band_of(ext, k, gather))
        hidden[...] = normed.astype(B16)
        for n in range(3):
            packed[rows, pl.ds(D * n, D)] = dot(hidden[...], w_qkv[:, pl.ds(D * n, D)]).astype(B16)

    head_mask = (iota((4 * 64, 128), 0) >> 6) == (iota((4 * 64, 128), 1) >> 5)
    head_one = jnp.where(head_mask, 1.0, 0.0)
    head_b16 = head_one.astype(B16)

    def expand(values):
        return jnp.concatenate([values] * 4, axis=0) * head_b16

    def fold(values):
        kept = values * head_one
        return (kept[0:64] + kept[64:128]) + (kept[128:192] + kept[192:256])

    def lanes(n, g):
        return pl.ds(D * n + 128 * g, 128)

    def forward(w, carry):
        rows = pl.ds(pl.multiple_of(w * 64, 64), 64)
        valid = row_valid(place, a, (w >= ACROSS).astype(jnp.int32), iota((64, 1), 0))
        bias = jnp.where(valid, 0.0, NEGATIVE)
        for g in range(4):
            queries = expand(packed[rows, lanes(0, g)])
            scores = dot_nt(packed[rows, lanes(1, g)], queries) * FACTOR + bias
            raised = jnp.exp(scores - jnp.max(scores, axis=0, keepdims=True))
            prob = raised * (1.0 / jnp.sum(raised, axis=0, keepdims=True))
            probs[w, g] = prob
            output = dot_tn(prob.astype(B16), packed[rows, lanes(2, g)])
            attended[rows, pl.ds(128 * g, 128)] = fold(output).astype(B16)
        return carry

    lax.fori_loop(0, 2 * ACROSS, forward, 0)

    own_attended = dot(scatter[...], attended[...]).astype(B16)
    own_both[pl.ds(CELLS, CELLS)] = own_attended
    own_out = (own_tokens + dot(own_attended, w_proj[...])).astype(B16)
    skip_out[...] = dot(to_rows, own_out).astype(B16)
    merged_in = own_out.astype(F32)
    quarters = [merged_in[MERGED * n : MERGED * (n + 1)] for n in range(4)]
    wide = 1.0 / (4 * D)

    def mean(values):
        return sum(jnp.sum(v, axis=-1, keepdims=True) for v in values) * wide

    center_at = mean(quarters)
    centers = [q - center_at for q in quarters]
    merged_inverse = lax.rsqrt(mean([c * c for c in centers]) + EPSILON)
    merged_normed = [c * merged_inverse for c in centers]
    back_mean = mean(merged_back)
    back_dot = mean([g * n for g, n in zip(merged_back, merged_normed)])
    for n in range(4):
        rows = pl.ds(MERGED * n, MERGED)
        merged_hidden[:, pl.ds(D * n, D)] = merged_normed[n].astype(B16)
        delta = merged_inverse * (merged_back[n] - back_mean - merged_normed[n] * back_dot)
        total_grad[rows] = (own_skip[MERGED * n : MERGED * (n + 1)] + delta).astype(B16)

    own_grad = dot_nt(total_grad[...], w_proj[...]).astype(B16)
    grad_own[...] = dot(to_rows, own_grad).astype(B16)
    edges_back[...] = dot(pick_edges, grad_own[...]).astype(B16)
    back_halo = Halo(place, ext_back, edges_back, halo_back_send, halo_back_recv)
    back_halo.start(grad_own)
    ext_back[pl.ds(CELLS, CELLS)] = grad_own[...]

    def merge_parts(i, carry):
        yhi, half = i // 2, i % 2
        columns = pl.ds(pl.multiple_of(i * 256, 256), 256)
        left = merged_grad[:, columns]
        for n in range(4):
            block = dot_tn(left, merged_hidden[:, pl.ds(D * n, D)]).astype(B16)
            for m in range(4):
                parts_merge[n, m // 2, m % 2, yhi, pl.ds(half * 4, 4)] = block[
                    :, 128 * m : 128 * (m + 1)
                ].reshape(4, 64, 128)
        return carry

    lax.fori_loop(0, 4, merge_parts, 0)
    merge_sum.start_core()
    merged_out[...] = dot(merged_hidden[...], w_merge[...]).astype(B16)
    transposed = own_both[...].T

    back_halo.wait()
    for k in range(2):
        values = band_of(ext_back, k, gather)
        valid = row_valid(place, a, k, iota((BAND, 1), 0))
        back_in[pl.ds(BAND * k, BAND)] = jnp.where(valid, values, 0.0).astype(B16)

    def backward(w, carry):
        rows = pl.ds(pl.multiple_of(w * 64, 64), 64)
        for g in range(4):
            queries = expand(packed[rows, lanes(0, g)])
            upstream = expand(back_in[rows, pl.ds(128 * g, 128)])
            key_rows, value_rows = packed[rows, lanes(1, g)], packed[rows, lanes(2, g)]
            prob = probs[w, g]
            prob_grad = dot_nt(value_rows, upstream)
            total = jnp.sum(prob * prob_grad, axis=0, keepdims=True)
            score_grad = (prob * (prob_grad - total) * FACTOR).astype(B16)
            packed_grad[rows, lanes(0, g)] = fold(dot_tn(score_grad, key_rows)).astype(B16)
            packed_grad[rows, lanes(1, g)] = dot(score_grad, queries).astype(B16)
            packed_grad[rows, lanes(2, g)] = dot(prob.astype(B16), upstream).astype(B16)
        return carry

    lax.fori_loop(0, 3, backward, 0)
    for h in range(2):
        merge_sum.add_core(h)
        merge_sum.start_first(h)
    lax.fori_loop(3, 2 * ACROSS, backward, 0)

    def widen(n):
        return (n // 96) * 128 + n % 96

    widen_fine = one_hot(384, 512, widen)
    widen_proj = one_hot(128, 512, lambda n: (n >> 5) * 128 + 96 + (n & 31))
    for n in range(3):
        columns = pl.ds(D * n, D)
        packed[pl.ds(0, CELLS), columns] = dot(scatter[...], packed_grad[:, columns]).astype(B16)
    own_packed = packed[pl.ds(0, CELLS)]
    for n in range(4):
        columns = pl.ds(512 * n, 512)
        spread[pl.ds(0, CELLS), columns] = dot(
            own_packed[:, 384 * n : 384 * (n + 1)], widen_fine
        ).astype(B16)
        spread[pl.ds(CELLS, CELLS), columns] = dot(
            total_grad[:, pl.ds(128 * n, 128)], widen_proj
        ).astype(B16)
    for r in range(YHI * ZS // 4):
        block = dot(transposed, spread[:, pl.ds(512 * r, 512)]).astype(B16)
        for m in range(4):
            lat = 4 * r + m
            parts_fine[:, :, :, lat // ZS, lat % ZS] = block[:, 128 * m : 128 * (m + 1)].reshape(
                XS, YLO, CORES, 32, 128
            )
    fine_sum.start_core()
    hidden_grad = dot_nt(own_packed, w_qkv[...])
    own_input = total_grad[...].astype(F32) + own_inverse * (
        hidden_grad
        - jnp.mean(hidden_grad, axis=-1, keepdims=True)
        - own_normed * jnp.mean(hidden_grad * own_normed, axis=-1, keepdims=True)
    )
    input_grad[...] = dot(to_rows, own_input.astype(B16)).astype(B16)

    for h in range(2):
        merge_sum.add_first(h)
        merge_sum.start_second(h)
    for h in range(2):
        fine_sum.add_core(h)
        fine_sum.start_first(h)
    for h in range(2):
        merge_sum.add_second(h)
    merge_sum.start_last()
    for h in range(2):
        fine_sum.add_first(h)
        fine_sum.start_second(h)
    merge_sum.add_last(sum_merge)
    for h in range(2):
        fine_sum.add_second(h)
    fine_sum.start_last()
    fine_sum.add_last(sum_fine)


def on_device(tokens, w_qkv, w_proj, w_merge, skip_grad, merged_grad, window_shift):
    vmem, smem = pltpu.VMEM, pltpu.SMEM
    inside = pl.BlockSpec(memory_space=vmem)
    outside = pl.BlockSpec(memory_space=pl.ANY)
    windows = 2 * ACROSS
    skip_out, merged_out, input_grad, sum_merge, sum_fine = pl.pallas_call(
        section_kernel,
        out_shape=[
            jax.ShapeDtypeStruct((CELLS, D), B16),
            jax.ShapeDtypeStruct((MERGED, D2), B16),
            jax.ShapeDtypeStruct((CELLS, D), B16),
            jax.ShapeDtypeStruct((64, 128), F32),
            jax.ShapeDtypeStruct((32, 128), F32),
        ],
        in_specs=[pl.BlockSpec(memory_space=smem)] + [inside] * 3 + [outside] * 3,
        out_specs=[inside] * 5,
        scratch_shapes=[
            vmem((D, 3 * D), B16),
            vmem((D, D), B16),
            vmem((4 * D, D2), B16),
            pltpu.SemaphoreType.DMA((3,)),
            vmem((SOURCES, D), B16),
            vmem((SOURCES, D), B16),
            vmem((2 * EDGE, D), B16),
            vmem((2 * EDGE, D), B16),
            vmem((CELLS, D), B16),
            pltpu.SemaphoreType.DMA((8,)),
            pltpu.SemaphoreType.DMA((8,)),
            pltpu.SemaphoreType.DMA((8,)),
            pltpu.SemaphoreType.DMA((8,)),
            vmem((BAND, 2 * CELLS + 4 * EDGE), B16),
            vmem((CELLS, 2 * BAND), B16),
            vmem((BAND, D), B16),
            vmem((2 * BAND, 3 * D), B16),
            vmem((windows, 4, 64, 256), F32),
            vmem((2 * BAND, D), B16),
            vmem((2 * BAND, D), B16),
            vmem((2 * BAND, 3 * D), B16),
            vmem((2 * CELLS, D), B16),
            vmem((2 * CELLS, YHI * ZS * 128), B16),
            vmem((MERGED, 4 * D), B16),
            vmem((CELLS, D), B16),
            vmem((XS, YLO, CORES, YHI, ZS, 64, 128), B16),
            vmem((XS, YLO, CORES, YHI, ZS, 32, 128), B16),
        ]
        + sum_scratch(64)
        + sum_scratch(32),
        compiler_params=pltpu.CompilerParams(
            collective_id=0, has_side_effects=True, vmem_limit_bytes=56 * 2**20
        ),
    )(
        window_shift,
        tokens.reshape(CELLS, D),
        skip_grad.reshape(CELLS, D),
        merged_grad.reshape(MERGED, D2),
        w_qkv,
        w_proj,
        w_merge,
    )
    return (
        skip_out.reshape(ROWS, COLS, D),
        merged_out.reshape(ROWS // 2, COLS // 2, D2),
        input_grad.reshape(ROWS, COLS, D),
        sum_fine[:, :96],
        sum_fine[:, 96:],
        sum_merge.T,
    )


def solution(mesh):
    in_specs = (
        P("lat", "lon", None),
        P(),
        P(),
        P(),
        P("lat", "lon", None),
        P("lat", "lon", None),
        P(),
    )
    out_specs = (
        P("lat", "lon", None),
        P("lat", "lon", None),
        P("lat", "lon", None),
        P("lon", "lat"),
        P("lon", "lat"),
        P("lon", "lat"),
    )
    return jax.shard_map(
        on_device, mesh=mesh, in_specs=in_specs, out_specs=out_specs, check_vma=False
    )
```

time: 297 us -> 96.5 us (0.32); the launches traced: 292 us -> 95.7 us
  local copies, waits for them, and re-layouts: 122 us -> 9 us
  matrix products: 49.8 us -> 0 us
  Pallas kernels: 47.3 us -> 86.1 us
  other arithmetic: 25.7 us -> 0 us
  waiting for transfers between devices: 23.1 us -> 0 us
  starting transfers between devices: 16.5 us -> 0 us
  between operations: 8.16 us -> 0.65 us
    dot_general x15 -> x0, matrix products: 49.8 us -> none  [the longest x1 10.3 us: attend_back(): jnp.einsum('nhqk,nqhd->nkhd', score_grad, queries, preferred_element_type...]
    reshape x9 -> x0, local copies, waits for them, and re-layouts: 39.4 us -> none  [the longest x2 21.9 us: on_device(): merge_block = merge_part.astype(jnp.bfloat16).reshape(XS, YLO, CORES, 128...]
    pallas_call x1, Pallas kernels: 47.3 us -> 86.1 us  [on_device(): pl.pallas_call(section_kernel, out_shape=[jax.ShapeDtypeStruct((CELLS, D)...]
    ppermute x8 -> x0, waiting for transfers between devices: 23.1 us -> none  [the longest x4 19.9 us: with_halo(): before = lax.ppermute(last, axis, up)]
    ppermute x8 -> x0, starting transfers between devices: 16.5 us -> none  [the longest x4 14 us: with_halo(): after = lax.ppermute(leading, axis, down)]
    transpose x10 -> x0, local copies, waits for them, and re-layouts: 15.8 us -> none  [the longest x1 4.46 us: attend_back(): jnp.einsum('nhqk,nqhd->nkhd', score_grad, queries, preferred_element_type...]
    another operation x3 -> x0, local copies, waits for them, and re-layouts: 14.5 us -> none  [the longest x2 7.45 us: attend_back(): grad_out = upstream.reshape(queries.shape)]
    concatenate x3 -> x0, local copies, waits for them, and re-layouts: 14.1 us -> none  [attend_back(): jnp.concatenate([query_grad.reshape(windows, per_window, -1), key_grad.re...]
  transfers between devices with their start and end apart: 8 -> 0, of which waited for: 4 -> 0; matrix products, arithmetic and copies ran while one was open for 14% -> 0% of each run, Pallas kernels for 0% -> 0%
where the time goes in v2:
time: 96.5 us; the launch traced here: 95.7 us
  Pallas kernels  86.1 us (89%)
  local copies, waits for them, and re-layouts  9 us (9%)
    pallas_call x1, Pallas kernels, on_device(): pl.pallas_call(section_kernel, out_shape=[jax.ShapeDtypeStruct((CELLS, D)...  86.1 us
    unnamed x5, local copies, waits for them, and re-layouts  7.6 us

profile of v2, /device:TPU:4, one launch (start us, length us, event | category | flops | bytes accessed | tf_op | source)
XLA Modules:
  0.0 95.7 jit_solution(14303336067853160396)
XLA Ops:
  0.6 86.1 %shard_map.118 = (bf16[256,512]{1,0:T(8,128)(2,1)}, bf16[64,1024]{1,0:T(8,128)(2,1)}, bf16[256,512]{1,0:T(8,128)(2,1)}, f32[64,128]{1,0:T(8,128)}, f32[32,128]{1,0:T(8,128)}) custom-call(s32[2]{0:T(128)} %shift.1, bf16[256,512]{1,0:T(8,128)(2,1)} %bitcast.8, bf16[256,512]{1,0:T(8,128)(2,1)} %bitcast.9, bf16[64,1024]{1,0:T(8,128)(2,1)} %bitcast.12, ...), custom_call_target="tpu_custom_call" | custom-call | tf_op jit(solution)/shard_map/pallas_call | solution.py:631
  86.7 1.4 %slice.7 = f32[32,32]{1,0:T(8,128)} slice(f32[32,128]{1,0:T(8,128)} %get-tuple-element.14), slice={[0:32], [96:128]} | slice | bytes 8192 | tf_op jit(solution)/shard_map/slice | solution.py:690
  88.1 1.7 %copy.18 = bf16[8,32,512]{2,1,0:T(8,128)(2,1)} copy(bf16[8,32,512]{2,1,0:T(8,128)(2,1)} %bitcast.11) | data formatting | bytes 524288
  89.8 1.6 %copy.19 = bf16[4,16,1024]{2,1,0:T(8,128)(2,1)} copy(bf16[4,16,1024]{2,1,0:T(8,128)(2,1)} %bitcast.13) | data formatting | bytes 262144
  91.3 1.7 %copy.20 = bf16[8,32,512]{2,1,0:T(8,128)(2,1)} copy(bf16[8,32,512]{2,1,0:T(8,128)(2,1)} %bitcast.10) | data formatting | bytes 524288
  93.0 1.3 %copy.21 = f32[32,96]{1,0:T(8,128)} copy(f32[32,96]{1,0:T(8,128)} %bitcast.14) | data formatting | bytes 24576
  94.3 1.4 %copy.22 = f32[128,64]{0,1:T(8,128)} copy(f32[128,64]{0,1:T(8,128)} %bitcast.15) | data formatting | bytes 65536

commit v3 on v2

v3 whole, which is shorter than its diff:
```python
import jax
import jax.numpy as jnp
from jax import lax
from jax.experimental import pallas as pl
from jax.experimental.pallas import tpu as pltpu
from jax.sharding import PartitionSpec as P

HEADS = 16
WIN = 8
EPSILON = 1e-05
NEGATIVE = -1e30
D = 512
D2 = 1024
ROWS, COLS = 8, 32
CELLS = ROWS * COLS
WINDOWS = COLS // WIN
FACTOR = 32 ** (-0.5)
MERGED = CELLS // 4
FRINGE = 384
F32, B16 = jnp.float32, jnp.bfloat16

XS, YLO, CORES, YHI, ZS = 4, 2, 2, 2, 8
YS = YLO * YHI
MESH = pl.DeviceIdType.MESH


class Place:
    def __init__(self):
        lon = lax.axis_index("lon")
        lat = lax.axis_index("lat")
        self.lon, self.lat = lon, lat
        self.core = lon % CORES
        self.ylo = (lon // CORES) % YLO
        self.x = lon // (CORES * YLO)
        self.z = lat % ZS
        self.yhi = lat // ZS

    def at(self, x=None, ylo=None, core=None, yhi=None, z=None):
        x = self.x if x is None else x
        ylo = self.ylo if ylo is None else ylo
        core = self.core if core is None else core
        yhi = self.yhi if yhi is None else yhi
        z = self.z if z is None else z
        return ((x * YLO + ylo) * CORES + core, yhi * ZS + z)

    def beside(self, dlat, dlon):
        lons, lats = XS * YLO * CORES, YHI * ZS
        return ((self.lon + dlon) % lons, (self.lat + dlat) % lats)

    def sibling(self):
        return self.at(core=1 - self.core)

    def x_step(self, k):
        return (self.x + k) % XS

    def y_step(self, k):
        y = (self.yhi * YLO + self.ylo + k) % YS
        return (y // YLO, y % YLO)

    def z_step(self, k):
        return (self.z + k) % ZS

    def core_step(self, f):
        return 1 - self.core if f else self.core

    def partners(self):
        out = [self.sibling()]
        for k in range(1, XS):
            out += [self.at(x=self.x_step(k), core=self.core_step(f)) for f in range(2)]
        for k in range(1, YS):
            yhi, ylo = self.y_step(k)
            out += [self.at(yhi=yhi, ylo=ylo, core=self.core_step(f)) for f in range(2)]
        out += [self.at(z=self.z_step(k)) for k in range(1, ZS)]
        for dlat in (-1, 0, 1):
            for dlon in (-1, 0, 1):
                if (dlat, dlon) != (0, 0):
                    out.append(self.beside(dlat, dlon))
        return out


def device_of(pair):
    return {"lon": pair[0], "lat": pair[1]}


def greet(partners):
    barrier = pltpu.get_barrier_semaphore()
    for pair in partners:
        pl.semaphore_signal(barrier, inc=1, device_id=device_of(pair), device_id_type=MESH)


def await_greetings(partners):
    pl.semaphore_wait(pltpu.get_barrier_semaphore(), len(partners))


HALF = ZS // 2


class Copies:
    def __init__(self, place, send, recv):
        self.place, self.send, self.recv = place, send, recv
        self.used = 0
        self.flying = {}

    def copy(self, src, dst, pair):
        slot = self.used
        self.used += 1
        made = pltpu.make_async_remote_copy(
            src_ref=src,
            dst_ref=dst,
            send_sem=self.send.at[slot],
            recv_sem=self.recv.at[slot],
            device_id=device_of(pair),
            device_id_type=MESH,
        )
        made.start()
        return made

    def wait(self, name):
        for made in self.flying[name]:
            made.wait()


def late_scratch(rows):
    copies = (XS - 1) + (YS - 1) + (ZS - 1)
    return [
        pltpu.VMEM((YLO, YHI, HALF, rows, 128), B16),
        pltpu.VMEM((XS, HALF, rows, 128), B16),
        pltpu.VMEM((YS - 1, HALF, rows, 128), B16),
        pltpu.VMEM((XS - 1, HALF, rows, 128), B16),
        pltpu.VMEM((ZS, rows, 128), B16),
        pltpu.VMEM((ZS - 1, rows, 128), B16),
        pltpu.SemaphoreType.DMA((copies,)),
        pltpu.SemaphoreType.DMA((copies,)),
    ]


def early_scratch(rows):
    copies = 2 + (XS - 1) + (YS - 1)
    return [
        pltpu.VMEM((XS, YLO, YHI, ZS, rows, 128), B16),
        pltpu.VMEM((XS - 1, YLO, YHI, HALF, rows, 128), B16),
        pltpu.VMEM((YS - 1, XS, HALF, rows, 128), B16),
        pltpu.SemaphoreType.DMA((copies,)),
        pltpu.SemaphoreType.DMA((copies,)),
    ]


class Late(Copies):
    def __init__(self, place, scratch):
        (self.sum_x, self.sum_y, self.late_y, self.late_x, self.column, self.from_z) = scratch[:6]
        super().__init__(place, *scratch[6:])

    def start_second(self, h):
        place = self.place
        if h == 0:
            self.flying["late_y"] = []
            for k in range(1, YS):
                yhi, ylo = place.y_step(k)
                self.flying["late_y"].append(
                    self.copy(
                        self.sum_x.at[ylo, yhi],
                        self.late_y.at[k - 1],
                        place.at(yhi=yhi, ylo=ylo),
                    )
                )
        else:
            self.flying["late_x"] = [
                self.copy(
                    self.sum_y.at[place.x_step(k)],
                    self.late_x.at[k - 1],
                    place.at(x=place.x_step(k)),
                )
                for k in range(1, XS)
            ]

    def add_second(self, h):
        place = self.place
        self.wait("late_y" if h == 0 else "late_x")
        if h == 0:
            total = self.sum_x[place.ylo, place.yhi].astype(F32)
            for k in range(YS - 1):
                total += self.late_y[k].astype(F32)
        else:
            total = self.sum_y[place.x].astype(F32)
            for k in range(XS - 1):
                total += self.late_x[k].astype(F32)
        self.column[pl.ds(h * HALF, HALF)] = total.astype(B16)

    def start_last(self):
        place = self.place
        self.flying["z"] = [
            self.copy(
                self.column.at[place.z_step(k)],
                self.from_z.at[k - 1],
                place.at(z=place.z_step(k)),
            )
            for k in range(1, ZS)
        ]

    def add_last(self, out):
        self.wait("z")
        total = self.column[self.place.z].astype(F32)
        for k in range(ZS - 1):
            total += self.from_z[k].astype(F32)
        out[...] = total


class Early(Copies):
    def __init__(self, place, parts, late, scratch):
        self.kept, self.from_x, self.from_y = scratch[:3]
        self.parts, self.late = parts, late
        super().__init__(place, *scratch[3:])

    def start_core(self):
        other = 1 - self.place.core
        self.flying["core"] = [
            self.copy(
                self.parts.at[:, :, other, :, pl.ds(h * HALF, HALF)],
                self.kept.at[:, :, :, pl.ds(h * HALF, HALF)],
                self.place.sibling(),
            )
            for h in range(2)
        ]

    def add_core(self, h):
        core = self.place.core
        self.flying["core"][h].wait()

        def body(i, carry):
            x, rest = i // (YLO * YHI), i % (YLO * YHI)
            ylo, yhi = rest // YHI, rest % YHI
            zs = pl.ds(h * HALF, HALF)
            own = self.parts[x, ylo, core, yhi, zs].astype(F32)
            got = self.kept[x, ylo, yhi, zs].astype(F32)
            self.kept[x, ylo, yhi, zs] = (own + got).astype(B16)
            return carry

        lax.fori_loop(0, XS * YLO * YHI, body, 0)

    def start_first(self, h):
        place = self.place
        zs = pl.ds(h * HALF, HALF)
        if h == 0:
            self.flying["x"] = [
                self.copy(
                    self.kept.at[place.x_step(k), :, :, zs],
                    self.from_x.at[k - 1],
                    place.at(x=place.x_step(k)),
                )
                for k in range(1, XS)
            ]
        else:
            self.flying["y"] = []
            for k in range(1, YS):
                yhi, ylo = place.y_step(k)
                self.flying["y"].append(
                    self.copy(
                        self.kept.at[:, ylo, yhi, zs],
                        self.from_y.at[k - 1],
                        place.at(yhi=yhi, ylo=ylo),
                    )
                )

    def add_first(self, h):
        place, late = self.place, self.late
        zs = pl.ds(h * HALF, HALF)
        self.wait("x" if h == 0 else "y")
        if h == 0:

            def body(i, carry):
                ylo, yhi = i // YHI, i % YHI
                total = self.kept[place.x, ylo, yhi, zs].astype(F32)
                for k in range(XS - 1):
                    total += self.from_x[k, ylo, yhi].astype(F32)
                late.sum_x[ylo, yhi] = total.astype(B16)
                return carry

            lax.fori_loop(0, YLO * YHI, body, 0)
        else:

            def body(x, carry):
                total = self.kept[x, place.ylo, place.yhi, zs].astype(F32)
                for k in range(YS - 1):
                    total += self.from_y[k, x].astype(F32)
                late.sum_y[x] = total.astype(B16)
                return carry

            lax.fori_loop(0, XS, body, 0)


def gather_scratch():
    copies = 4 * (2 * XS - 1)
    return [
        pltpu.VMEM((2 * XS, MERGED, D), B16),
        pltpu.VMEM((2 * YS, MERGED, D // 2), B16),
        pltpu.VMEM((2 * XS, MERGED, D // 2), B16),
        pltpu.VMEM((2 * YS, MERGED, D), B16),
        pltpu.VMEM((YHI, MERGED, D // 2), B16),
        pltpu.VMEM((XS, CORES, MERGED, D // 2), B16),
        pltpu.VMEM((YLO, CORES, MERGED, D), B16),
        pltpu.SemaphoreType.DMA((copies,)),
        pltpu.SemaphoreType.DMA((copies,)),
    ]


class Gather(Copies):
    def __init__(self, place, scratch):
        (self.grad_x, self.grad_y, self.hidden_x, self.hidden_y) = scratch[:4]
        (self.grad_parts, self.hidden_parts_x, self.hidden_parts_y) = scratch[4:7]
        super().__init__(place, *scratch[7:])

    def around(self):
        return [(k, f) for k in range(XS) for f in range(2) if (k, f) != (0, 0)]

    def start_grads(self, grads):
        place = self.place
        quarter = D // 2
        self.grad_x[0, :, 0:quarter] = grads[:, 0:quarter]
        self.grad_x[0, :, quarter:D] = grads[:, D : D + quarter]
        for yhi in range(YHI):
            start = yhi * D + quarter
            self.grad_parts[yhi] = grads[:, start : start + quarter]
        self.grad_y[0] = self.grad_parts[place.yhi]
        self.flying["grads"] = []
        for k, f in self.around():
            pair = place.at(x=place.x_step(k), core=place.core_step(f))
            self.flying["grads"].append(
                self.copy(self.grad_x.at[0], self.grad_x.at[2 * k + f], pair)
            )
            yhi, ylo = place.y_step(k)
            pair = place.at(yhi=yhi, ylo=ylo, core=place.core_step(f))
            self.flying["grads"].append(
                self.copy(self.grad_parts.at[yhi], self.grad_y.at[2 * k + f], pair)
            )

    def start_hidden(self, hidden):
        place = self.place
        for x in range(XS):
            for ylo in range(YLO):
                for core in range(CORES):
                    start = ((x * YLO + ylo) * CORES + core) * 128
                    block = hidden[:, start : start + 128]
                    self.hidden_parts_x[x, core, :, 128 * ylo : 128 * (ylo + 1)] = block
                    self.hidden_parts_y[ylo, core, :, 128 * x : 128 * (x + 1)] = block
        self.flying["hidden_x"], self.flying["hidden_y"] = [], []
        for k, f in self.around():
            core = place.core_step(f)
            yhi, ylo = place.y_step(k)
            self.flying["hidden_y"].append(
                self.copy(
                    self.hidden_parts_y.at[ylo, core],
                    self.hidden_y.at[2 * k + f],
                    place.at(yhi=yhi, ylo=ylo, core=core),
                )
            )
            x = place.x_step(k)
            self.flying["hidden_x"].append(
                self.copy(
                    self.hidden_parts_x.at[x, core],
                    self.hidden_x.at[2 * k + f],
                    place.at(x=x, core=core),
                )
            )
        self.hidden_x[0] = self.hidden_parts_x[place.x, place.core]
        self.hidden_y[0] = self.hidden_parts_y[place.ylo, place.core]

    def sum_x(self, grads_t, late):
        self.wait("hidden_x")
        hidden = self.hidden_x[...].reshape(2 * XS * MERGED, D // 2)
        block = dot(grads_t[...], hidden).astype(B16)
        for ylo in range(YLO):
            late.sum_x[ylo] = block[:, 128 * ylo : 128 * (ylo + 1)].reshape(YHI, HALF, 64, 128)

    def sum_y(self, grads_t, late):
        self.wait("hidden_y")
        hidden = self.hidden_y[...].reshape(2 * YS * MERGED, D)
        block = dot(grads_t[...], hidden).astype(B16)
        for x in range(XS):
            late.sum_y[x] = block[:, 128 * x : 128 * (x + 1)].reshape(HALF, 64, 128)


def iota(shape, dim):
    return lax.broadcasted_iota(jnp.int32, shape, dim)


def one_hot(rows, cols, index):
    place = index(iota((rows, 1), 0))
    return jnp.where(iota((rows, cols), 1) == place, 1.0, 0.0).astype(B16)


def dot(a, b):
    return jnp.dot(a, b, preferred_element_type=F32)


def dot_nt(a, b):
    return lax.dot_general(a, b, (((1,), (1,)), ((), ())), preferred_element_type=F32)


def dot_tn(a, b):
    return lax.dot_general(a, b, (((0,), (0,)), ((), ())), preferred_element_type=F32)


def rows_at(n):
    return n >> 5, n & 31


def rows_index(i, j):
    return i * COLS + j


def merge_at(n):
    part, r, c = n >> 6, (n >> 4) & 3, n & 15
    return 2 * r + (part & 1), 2 * c + (part >> 1)


def merge_index(i, j):
    return (((j & 1) * 2 + (i & 1)) << 6) + ((i >> 1) << 4) + (j >> 1)


def window_at(n):
    return (n >> 3) & 7, ((n >> 6) << 3) + (n & 7)


def window_index(i, j):
    return ((j >> 3) << 6) + (i << 3) + (j & 7)


def fringe_at(n):
    side = n < 256
    m = n & 31
    strip = n < 320
    corner = n & 15
    second = jnp.where(n < 352, 0, 1)
    i_side = ((n >> 5) & 3) + jnp.where(n < 128, 0, 4)
    i = jnp.where(side, i_side, jnp.where(strip, m >> 2, (corner >> 2) + 4 * second))
    last = jnp.where(strip, jnp.where(n >= 288, 1, 0), (n >> 4) & 1)
    j = jnp.where(side, m, (n & 3) + last * (COLS - 4))
    return i, j


def around_index(index, i, j):
    up, down, left, right = i < 0, i >= ROWS, j < 0, j >= COLS
    row4 = jnp.where(up, i + 4, jnp.where(down, i - ROWS, i))
    col4 = jnp.where(left, j + 4, j - COLS)
    north = up | down
    side = north & ~(left | right)
    strip = (left | right) & ~north
    corner = north & (left | right)
    at = index(i, j)
    at = jnp.where(side, CELLS + jnp.where(up, 128, 0) + row4 * COLS + j, at)
    at = jnp.where(strip, CELLS + 256 + jnp.where(left, 32, 0) + row4 * 4 + col4, at)
    base = CELLS + 320 + jnp.where(up, 32, 0) + jnp.where(left, 16, 0)
    return jnp.where(corner, base + row4 * 4 + col4, at)


def normalize(values):
    center = values - jnp.mean(values, axis=-1, keepdims=True)
    inverse = lax.rsqrt(jnp.mean(center * center, axis=-1, keepdims=True) + EPSILON)
    return center * inverse, inverse


FRINGES = (
    (0, 128, -1, 0),
    (128, 128, 1, 0),
    (256, 32, 0, -1),
    (288, 32, 0, 1),
    (320, 16, -1, -1),
    (336, 16, -1, 1),
    (352, 16, 1, -1),
    (368, 16, 1, 1),
)


def around_scratch():
    return [
        pltpu.VMEM((CELLS + FRINGE, D), B16),
        pltpu.VMEM((FRINGE, D), B16),
        pltpu.SemaphoreType.DMA((len(FRINGES),)),
        pltpu.SemaphoreType.DMA((len(FRINGES),)),
    ]


class Around(Copies):
    def __init__(self, place, scratch):
        self.block, self.fringe = scratch[:2]
        super().__init__(place, *scratch[2:])

    def pick(self, values, picks):
        self.fringe[...] = dot(picks, values).astype(B16)

    def start(self, values):
        self.flying["fringe"] = [
            self.copy(
                self.fringe.at[pl.ds(offset, size)],
                self.block.at[pl.ds(CELLS + offset, size)],
                self.place.beside(dlat, dlon),
            )
            for offset, size, dlat, dlon in FRINGES
        ]
        self.block[pl.ds(0, CELLS)] = values

    def get(self, picks):
        self.wait("fringe")
        return dot(picks, self.block[...])


def section_kernel(
    shift,
    tokens,
    skip_grad,
    merged_grad,
    w_qkv_hbm,
    w_proj_hbm,
    w_merge_hbm,
    skip_out,
    merged_out,
    input_grad,
    sum_merge,
    sum_fine,
    w_qkv,
    w_proj,
    w_merge,
    load,
    to_back,
    to_windows,
    to_output,
    pick_window,
    pick_merge,
    normed,
    packed,
    probs,
    attended,
    window_total,
    packed_grad,
    both_t,
    spread,
    merged_hidden,
    total_grad,
    grads_x_t,
    grads_y_t,
    parts_fine,
    *scratch,
):
    place = Place()
    partners = place.partners()
    greet(partners)
    loads = [
        pltpu.make_async_copy(src, dst, load.at[n])
        for n, (src, dst) in enumerate(
            ((w_qkv_hbm, w_qkv), (w_proj_hbm, w_proj), (w_merge_hbm, w_merge))
        )
    ]
    for made in loads:
        made.start()
    rounds = [Around(place, scratch[4 * n : 4 * n + 4]) for n in range(4)]
    scratch = scratch[16:]
    factors = Gather(place, scratch[:9])
    merge_sum = Late(place, scratch[9:17])
    fine_late = Late(place, scratch[17:25])
    fine_sum = Early(place, parts_fine, fine_late, scratch[25:])

    a, b = shift[0], shift[1]
    down = jnp.where(a >= WIN // 2, a - WIN, a)
    right = jnp.where(b >= WIN // 2, b - WIN, b)

    def picker(index):
        return one_hot(FRINGE, CELLS, lambda n: index(*fringe_at(n)))

    def shifted(at, index, sign):
        def source(n):
            i, j = at(n)
            return around_index(index, i + sign * down, j + sign * right)

        return one_hot(CELLS, CELLS + FRINGE, source)

    rounds[0].pick(tokens[...], picker(rows_index))
    from_tokens = shifted(window_at, rows_index, 1)
    await_greetings(partners)
    rounds[0].start(tokens[...])
    factors.start_grads(merged_grad)

    to_back[...] = shifted(merge_at, window_index, -1)
    to_windows[...] = shifted(window_at, merge_index, 1)
    to_output[...] = shifted(rows_at, window_index, -1)
    pick_window[...] = picker(window_index)
    pick_merge[...] = picker(merge_index)
    to_merged = one_hot(CELLS, CELLS, lambda n: rows_index(*merge_at(n)))
    to_rows = one_hot(CELLS, CELLS, lambda n: merge_index(*rows_at(n)))
    own_tokens = dot(to_merged, tokens[...])
    own_skip = dot(to_merged, skip_grad[...])
    loads[0].wait()

    values, inverse = normalize(rounds[0].get(from_tokens))
    normed[...] = values
    hidden = values.astype(B16)
    for n in range(3):
        columns = pl.ds(D * n, D)
        packed[:, columns] = dot(hidden, w_qkv[:, columns]).astype(B16)

    head_mask = (iota((4 * 64, 128), 0) >> 6) == (iota((4 * 64, 128), 1) >> 5)
    head_one = jnp.where(head_mask, 1.0, 0.0)
    head_b16 = head_one.astype(B16)

    def expand(values):
        return jnp.concatenate([values] * 4, axis=0) * head_b16

    def fold(values):
        kept = values * head_one
        return (kept[0:64] + kept[64:128]) + (kept[128:192] + kept[192:256])

    def lanes(n, g):
        return pl.ds(D * n + 128 * g, 128)

    key_row = down + ((iota((64, 1), 0) >> 3) & 7)
    query_row = down + ((iota((1, 256), 1) >> 3) & 7)
    key_away = (key_row < 0) | (key_row >= ROWS)
    query_away = (query_row < 0) | (query_row >= ROWS)
    pole = place.lat == jnp.where(a >= WIN // 2, 0, YHI * ZS - 1)
    apart = jnp.where(key_away, 1, 0) != jnp.where(query_away, 1, 0)
    bias = jnp.where(apart, jnp.where(pole, NEGATIVE, 0.0), 0.0)

    def forward(w, carry):
        rows = pl.ds(pl.multiple_of(w * 64, 64), 64)
        for g in range(4):
            queries = expand(packed[rows, lanes(0, g)])
            scores = dot_nt(packed[rows, lanes(1, g)], queries) * FACTOR + bias
            raised = jnp.exp(scores - jnp.max(scores, axis=0, keepdims=True))
            prob = raised * (1.0 / jnp.sum(raised, axis=0, keepdims=True))
            probs[w, g] = prob
            output = dot_tn(prob.astype(B16), packed[rows, lanes(2, g)])
            attended[rows, pl.ds(128 * g, 128)] = fold(output).astype(B16)
        return carry

    lax.fori_loop(0, WINDOWS, forward, 0)
    rounds[1].pick(attended[...], pick_window[...])
    rounds[1].start(attended[...])

    loads[1].wait()
    loads[2].wait()
    merged_back = [
        dot_nt(merged_grad[...], w_merge[pl.ds(D * part, D)]) for part in range(4)
    ]
    both_t[:, pl.ds(0, CELLS)] = hidden.T
    both_t[:, pl.ds(CELLS, CELLS)] = attended[...].T
    factors.wait("grads")
    grads_x_t[...] = factors.grad_x[...].reshape(2 * XS * MERGED, D).T
    grads_y_t[...] = factors.grad_y[...].reshape(2 * YS * MERGED, D // 2).T

    own_attended = rounds[1].get(to_back[...]).astype(B16)
    own_out = (own_tokens + dot(own_attended, w_proj[...])).astype(B16)
    merged_in = own_out.astype(F32)
    quarters = [merged_in[MERGED * n : MERGED * (n + 1)] for n in range(4)]
    wide = 1.0 / (4 * D)

    def mean(values):
        return sum(jnp.sum(v, axis=-1, keepdims=True) for v in values) * wide

    center_at = mean(quarters)
    centers = [q - center_at for q in quarters]
    merged_inverse = lax.rsqrt(mean([c * c for c in centers]) + EPSILON)
    merged_normed = [c * merged_inverse for c in centers]
    back_mean = mean(merged_back)
    back_dot = mean([g * n for g, n in zip(merged_back, merged_normed)])
    for n in range(4):
        rows = pl.ds(MERGED * n, MERGED)
        merged_hidden[:, pl.ds(D * n, D)] = merged_normed[n].astype(B16)
        delta = merged_inverse * (merged_back[n] - back_mean - merged_normed[n] * back_dot)
        total_grad[rows] = (own_skip[MERGED * n : MERGED * (n + 1)] + delta).astype(B16)
    rounds[2].pick(total_grad[...], pick_merge[...])
    rounds[2].start(total_grad[...])
    factors.start_hidden(merged_hidden)

    skip_out[...] = dot(to_rows, own_out).astype(B16)
    merged_out[...] = dot(merged_hidden[...], w_merge[...]).astype(B16)

    window_total[...] = rounds[2].get(to_windows[...]).astype(B16)
    attended[...] = dot_nt(window_total[...], w_proj[...]).astype(B16)

    def backward(w, carry):
        rows = pl.ds(pl.multiple_of(w * 64, 64), 64)
        for g in range(4):
            queries = expand(packed[rows, lanes(0, g)])
            upstream = expand(attended[rows, pl.ds(128 * g, 128)])
            key_rows, value_rows = packed[rows, lanes(1, g)], packed[rows, lanes(2, g)]
            prob = probs[w, g]
            prob_grad = dot_nt(value_rows, upstream)
            total = jnp.sum(prob * prob_grad, axis=0, keepdims=True)
            score_grad = (prob * (prob_grad - total) * FACTOR).astype(B16)
            packed_grad[rows, lanes(0, g)] = fold(dot_tn(score_grad, key_rows)).astype(B16)
            packed_grad[rows, lanes(1, g)] = dot(score_grad, queries).astype(B16)
            packed_grad[rows, lanes(2, g)] = dot(prob.astype(B16), upstream).astype(B16)
        return carry

    lax.fori_loop(0, WINDOWS // 2, backward, 0)
    factors.sum_x(grads_x_t, merge_sum)
    merge_sum.start_second(0)
    factors.sum_y(grads_y_t, merge_sum)
    merge_sum.start_second(1)
    lax.fori_loop(WINDOWS // 2, WINDOWS, backward, 0)

    widen_fine = one_hot(384, 512, lambda n: (n // 96) * 128 + n % 96)
    widen_proj = one_hot(128, 512, lambda n: (n >> 5) * 128 + 96 + (n & 31))
    for n in range(4):
        columns = pl.ds(512 * n, 512)
        spread[pl.ds(0, CELLS), columns] = dot(
            packed_grad[:, pl.ds(384 * n, 384)], widen_fine
        ).astype(B16)
        spread[pl.ds(CELLS, CELLS), columns] = dot(
            window_total[:, pl.ds(128 * n, 128)], widen_proj
        ).astype(B16)
    for r in range(YHI * ZS // 4):
        block = dot(both_t[...], spread[:, pl.ds(512 * r, 512)]).astype(B16)
        for m in range(4):
            lat = 4 * r + m
            parts_fine[:, :, :, lat // ZS, lat % ZS] = block[:, 128 * m : 128 * (m + 1)].reshape(
                XS, YLO, CORES, 32, 128
            )
    fine_sum.start_core()
    merge_sum.add_second(0)
    merge_sum.add_second(1)
    merge_sum.start_last()
    for h in range(2):
        fine_sum.add_core(h)
        fine_sum.start_first(h)

    hidden_grad = dot_nt(packed_grad[...], w_qkv[...])
    window_input = window_total[...].astype(F32) + inverse * (
        hidden_grad
        - jnp.mean(hidden_grad, axis=-1, keepdims=True)
        - normed[...] * jnp.mean(hidden_grad * normed[...], axis=-1, keepdims=True)
    )
    window_input = window_input.astype(B16)
    rounds[3].pick(window_input, pick_window[...])
    rounds[3].start(window_input)

    for h in range(2):
        fine_sum.add_first(h)
        fine_late.start_second(h)
    merge_sum.add_last(sum_merge)
    for h in range(2):
        fine_late.add_second(h)
    fine_late.start_last()
    input_grad[...] = rounds[3].get(to_output[...]).astype(B16)
    fine_late.add_last(sum_fine)


def finish_kernel(sum_merge, sum_fine, *refs):
    for src, dst in zip(refs[:3], refs[3:6]):
        dst[...] = src[...]
    dw_qkv, dw_proj, dw_merge = refs[6:]
    dw_qkv[...] = sum_fine[:, 0:96]
    dw_proj[...] = sum_fine[:, 96:128]
    dw_merge[...] = sum_merge[...]


def on_device(tokens, w_qkv, w_proj, w_merge, skip_grad, merged_grad, window_shift):
    vmem, smem = pltpu.VMEM, pltpu.SMEM
    inside = pl.BlockSpec(memory_space=vmem)
    outside = pl.BlockSpec(memory_space=pl.ANY)
    shape = jax.ShapeDtypeStruct
    big = [shape((CELLS, D), B16), shape((MERGED, D2), B16), shape((CELLS, D), B16)]
    skip_out, merged_out, input_grad, sum_merge, sum_fine = pl.pallas_call(
        section_kernel,
        out_shape=big + [shape((64, 128), F32), shape((32, 128), F32)],
        in_specs=[pl.BlockSpec(memory_space=smem)] + [inside] * 3 + [outside] * 3,
        out_specs=[inside] * 5,
        scratch_shapes=[
            vmem((D, 3 * D), B16),
            vmem((D, D), B16),
            vmem((4 * D, D2), B16),
            pltpu.SemaphoreType.DMA((3,)),
            vmem((CELLS, CELLS + FRINGE), B16),
            vmem((CELLS, CELLS + FRINGE), B16),
            vmem((CELLS, CELLS + FRINGE), B16),
            vmem((FRINGE, CELLS), B16),
            vmem((FRINGE, CELLS), B16),
            vmem((CELLS, D), F32),
            vmem((CELLS, 3 * D), B16),
            vmem((WINDOWS, 4, 64, 256), F32),
            vmem((CELLS, D), B16),
            vmem((CELLS, D), B16),
            vmem((CELLS, 3 * D), B16),
            vmem((D, 2 * CELLS), B16),
            vmem((2 * CELLS, YHI * ZS * 128), B16),
            vmem((MERGED, 4 * D), B16),
            vmem((CELLS, D), B16),
            vmem((D, 2 * XS * MERGED), B16),
            vmem((D // 2, 2 * YS * MERGED), B16),
            vmem((XS, YLO, CORES, YHI, ZS, 32, 128), B16),
        ]
        + around_scratch() * 4
        + gather_scratch()
        + late_scratch(64)
        + late_scratch(32)
        + early_scratch(32),
        compiler_params=pltpu.CompilerParams(
            collective_id=0, has_side_effects=True, vmem_limit_bytes=56 * 2**20
        ),
    )(
        window_shift,
        tokens.reshape(CELLS, D),
        skip_grad.reshape(CELLS, D),
        merged_grad.reshape(MERGED, D2),
        w_qkv,
        w_proj,
        w_merge,
    )
    skip_out, merged_out, input_grad, dw_qkv, dw_proj, dw_merge = pl.pallas_call(
        finish_kernel,
        out_shape=big + [shape((32, 96), F32), shape((32, 32), F32), shape((64, 128), F32)],
        in_specs=[inside] * 5,
        out_specs=[inside] * 6,
    )(sum_merge, sum_fine, skip_out, merged_out, input_grad)
    return (
        skip_out.reshape(ROWS, COLS, D),
        merged_out.reshape(ROWS // 2, COLS // 2, D2),
        input_grad.reshape(ROWS, COLS, D),
        dw_qkv,
        dw_proj,
        dw_merge.T,
    )


def solution(mesh):
    in_specs = (
        P("lat", "lon", None),
        P(),
        P(),
        P(),
        P("lat", "lon", None),
        P("lat", "lon", None),
        P(),
    )
    out_specs = (
        P("lat", "lon", None),
        P("lat", "lon", None),
        P("lat", "lon", None),
        P("lon", "lat"),
        P("lon", "lat"),
        P("lon", "lat"),
    )
    return jax.shard_map(
        on_device, mesh=mesh, in_specs=in_specs, out_specs=out_specs, check_vma=False
    )
```

time: 96.5 us -> 75.8 us (0.79)
  Pallas kernels: 86.1 us -> 73.8 us
  local copies, waits for them, and re-layouts: 9 us -> 0 us
    pallas_call x1 -> x2, Pallas kernels: 86.1 us -> 73.8 us  [the longest x1 71.8 us: on_device(): pl.pallas_call(section_kernel, out_shape=big + [shape((64, 128), F32), sh...]
    unnamed x5 -> x0, local copies, waits for them, and re-layouts: 7.6 us -> none
    slice x1 -> x0, local copies, waits for them, and re-layouts: 1.4 us -> none  [on_device(): sum_fine[:, 96:]]
where the time goes in v3:
time: 75.8 us; the launch traced here: 74.4 us
  Pallas kernels  73.8 us (97%)
    pallas_call x1, Pallas kernels, on_device(): pl.pallas_call(section_kernel, out_shape=big + [shape((64, 128), F32), sh...  71.8 us
    pallas_call x1, Pallas kernels, on_device(): pl.pallas_call(finish_kernel, out_shape=big + [shape((32, 96), F32), shap...  1.98 us

profile of v3, /device:TPU:4, one launch (start us, length us, event | category | flops | bytes accessed | tf_op | source)
XLA Modules:
  0.0 74.4 jit_solution(1462384983369900381)
XLA Ops:
  0.6 71.8 %shard_map.118 = (bf16[256,512]{1,0:T(8,128)(2,1)}, bf16[64,1024]{1,0:T(8,128)(2,1)}, bf16[256,512]{1,0:T(8,128)(2,1)}, f32[64,128]{1,0:T(8,128)}, f32[32,128]{1,0:T(8,128)}) custom-call(s32[2]{0:T(128)} %shift.1, bf16[256,512]{1,0:T(8,128)(2,1)} %bitcast.7, bf16[256,512]{1,0:T(8,128)(2,1)} %bitcast.8, bf16[64,1024]{1,0:T(8,128)(2,1)} %bitcast.9, ...), custom_call_target="tpu_custom_call" | custom-call | tf_op jit(solution)/shard_map/pallas_call | solution.py:762
  72.4 2.0 %shard_map.119 = (bf16[256,512]{1,0:T(8,128)(2,1)}, bf16[64,1024]{1,0:T(8,128)(2,1)}, bf16[256,512]{1,0:T(8,128)(2,1)}, f32[32,96]{1,0:T(8,128)}, f32[32,32]{1,0:T(8,128)}, /*index=5*/f32[64,128]{1,0:T(8,128)}) custom-call(f32[64,128]{1,0:T(8,128)} %get-tuple-element.17.sum_merge, f32[32,128]{1,0:T(8,128)} %get-tuple-element.18.sum_fine, ...), custom_call_target="tpu_custom_call" | custom-call | tf_op jit(solution)/shard_map/pallas_call | solution.py:808

commit v4 on v3

v4 whole, which is shorter than its diff:
```python
import functools

import jax
import jax.numpy as jnp
from jax import lax
from jax.experimental import pallas as pl
from jax.experimental.pallas import tpu as pltpu
from jax.sharding import PartitionSpec as P

HEADS = 16
WIN = 8
EPSILON = 1e-05
NEGATIVE = -1e30
D = 512
D2 = 1024
ROWS, COLS = 8, 32
CELLS = ROWS * COLS
WINDOWS = COLS // WIN
FACTOR = 32 ** (-0.5)
MERGED = CELLS // 4
F32, B16 = jnp.float32, jnp.bfloat16

XS, YLO, CORES, YHI, ZS = 4, 2, 2, 2, 8
YS = YLO * YHI
MESH = pl.DeviceIdType.MESH


class Place:
    def __init__(self):
        lon = lax.axis_index("lon")
        lat = lax.axis_index("lat")
        self.lon, self.lat = lon, lat
        self.core = lon % CORES
        self.ylo = (lon // CORES) % YLO
        self.x = lon // (CORES * YLO)
        self.z = lat % ZS
        self.yhi = lat // ZS

    def at(self, x=None, ylo=None, core=None, yhi=None, z=None):
        x = self.x if x is None else x
        ylo = self.ylo if ylo is None else ylo
        core = self.core if core is None else core
        yhi = self.yhi if yhi is None else yhi
        z = self.z if z is None else z
        return ((x * YLO + ylo) * CORES + core, yhi * ZS + z)

    def beside(self, dlat, dlon):
        lons, lats = XS * YLO * CORES, YHI * ZS
        return ((self.lon + dlon) % lons, (self.lat + dlat) % lats)

    def sibling(self):
        return self.at(core=1 - self.core)

    def x_step(self, k):
        return (self.x + k) % XS

    def y_step(self, k):
        y = (self.yhi * YLO + self.ylo + k) % YS
        return (y // YLO, y % YLO)

    def z_step(self, k):
        return (self.z + k) % ZS

    def core_step(self, f):
        return 1 - self.core if f else self.core

    def partners(self):
        out = [self.sibling()]
        for k in range(1, XS):
            out += [self.at(x=self.x_step(k), core=self.core_step(f)) for f in range(2)]
        for k in range(1, YS):
            yhi, ylo = self.y_step(k)
            out += [self.at(yhi=yhi, ylo=ylo, core=self.core_step(f)) for f in range(2)]
        out += [self.at(z=self.z_step(k)) for k in range(1, ZS)]
        for dlat in (-1, 0, 1):
            for dlon in (-1, 0, 1):
                if (dlat, dlon) != (0, 0):
                    out.append(self.beside(dlat, dlon))
        return out


def device_of(pair):
    return {"lon": pair[0], "lat": pair[1]}


def greet(partners):
    barrier = pltpu.get_barrier_semaphore()
    for pair in partners:
        pl.semaphore_signal(barrier, inc=1, device_id=device_of(pair), device_id_type=MESH)


def await_greetings(partners):
    pl.semaphore_wait(pltpu.get_barrier_semaphore(), len(partners))


HALF = ZS // 2


class Copies:
    def __init__(self, place, send, recv):
        self.place, self.send, self.recv = place, send, recv
        self.used = 0
        self.flying = {}

    def copy(self, src, dst, pair):
        slot = self.used
        self.used += 1
        made = pltpu.make_async_remote_copy(
            src_ref=src,
            dst_ref=dst,
            send_sem=self.send.at[slot],
            recv_sem=self.recv.at[slot],
            device_id=device_of(pair),
            device_id_type=MESH,
        )
        made.start()
        return made

    def wait(self, name):
        for made in self.flying[name]:
            made.wait()


def path_scratch(rows, first, second):
    one, two = first[0], second
    flat = 1
    for size in two:
        flat *= size
    copies = (first[1] - 1) + (flat - 1)
    out = [
        pltpu.VMEM((*two, rows, 128), B16),
        pltpu.VMEM((flat - 1, rows, 128), B16),
        pltpu.SemaphoreType.DMA((copies,)),
        pltpu.SemaphoreType.DMA((copies,)),
    ]
    if one:
        out += [
            pltpu.VMEM((XS, YLO, YHI, rows, 128), B16),
            pltpu.VMEM((first[1] - 1, *two, rows, 128), B16),
        ]
    return out


class PathXY(Copies):
    def __init__(self, place, scratch):
        self.sum, self.late = scratch[:2]
        super().__init__(place, *scratch[2:4])
        if len(scratch) > 4:
            self.parts, self.got = scratch[4:]

    def start_first(self):
        place = self.place
        self.flying["x"] = [
            self.copy(
                self.parts.at[place.x_step(k)], self.got.at[k - 1], place.at(x=place.x_step(k))
            )
            for k in range(1, XS)
        ]

    def add_first(self):
        self.wait("x")
        for ylo in range(YLO):
            for yhi in range(YHI):
                total = self.parts[self.place.x, ylo, yhi].astype(F32)
                for k in range(XS - 1):
                    total += self.got[k, ylo, yhi].astype(F32)
                self.sum[ylo, yhi] = total.astype(B16)

    def start_second(self):
        self.flying["y"] = []
        for k in range(1, YS):
            yhi, ylo = self.place.y_step(k)
            pair = self.place.at(yhi=yhi, ylo=ylo)
            self.flying["y"].append(self.copy(self.sum.at[ylo, yhi], self.late.at[k - 1], pair))

    def add_second(self):
        self.wait("y")
        total = self.sum[self.place.ylo, self.place.yhi].astype(F32)
        for k in range(YS - 1):
            total += self.late[k].astype(F32)
        return total.astype(B16)


class PathYX(Copies):
    def __init__(self, place, scratch):
        self.sum, self.late = scratch[:2]
        super().__init__(place, *scratch[2:4])
        self.parts, self.got = scratch[4:]

    def start_first(self):
        self.flying["y"] = []
        for k in range(1, YS):
            yhi, ylo = self.place.y_step(k)
            pair = self.place.at(yhi=yhi, ylo=ylo)
            self.flying["y"].append(
                self.copy(self.parts.at[:, ylo, yhi], self.got.at[k - 1], pair)
            )

    def add_first(self):
        self.wait("y")
        for x in range(XS):
            total = self.parts[x, self.place.ylo, self.place.yhi].astype(F32)
            for k in range(YS - 1):
                total += self.got[k, x].astype(F32)
            self.sum[x] = total.astype(B16)

    def start_second(self):
        place = self.place
        self.flying["x"] = [
            self.copy(
                self.sum.at[place.x_step(k)], self.late.at[k - 1], place.at(x=place.x_step(k))
            )
            for k in range(1, XS)
        ]

    def add_second(self):
        self.wait("x")
        total = self.sum[self.place.x].astype(F32)
        for k in range(XS - 1):
            total += self.late[k].astype(F32)
        return total.astype(B16)


def last_scratch(rows):
    return [
        pltpu.VMEM((ZS, rows, 128), B16),
        pltpu.VMEM((ZS - 1, rows, 128), B16),
        pltpu.SemaphoreType.DMA((ZS - 1,)),
        pltpu.SemaphoreType.DMA((ZS - 1,)),
    ]


class Last(Copies):
    def __init__(self, place, scratch):
        self.column, self.from_z = scratch[:2]
        super().__init__(place, *scratch[2:])

    def start(self):
        place = self.place
        self.flying["z"] = [
            self.copy(
                self.column.at[place.z_step(k)],
                self.from_z.at[k - 1],
                place.at(z=place.z_step(k)),
            )
            for k in range(1, ZS)
        ]

    def add(self, out):
        self.wait("z")
        total = self.column[self.place.z].astype(F32)
        for k in range(ZS - 1):
            total += self.from_z[k].astype(F32)
        out[...] = total


def share_scratch():
    half = D // 2
    return [
        pltpu.VMEM((2, half, CELLS), B16),
        pltpu.VMEM((2, half, CELLS), B16),
        pltpu.VMEM((2, half, CELLS), B16),
        pltpu.VMEM((CELLS, D), B16),
        pltpu.VMEM((CELLS, 3 * D), B16),
        pltpu.SemaphoreType.DMA((5,)),
        pltpu.SemaphoreType.DMA((5,)),
    ]


class Share(Copies):
    def __init__(self, place, scratch):
        self.out, self.hidden, self.attended, self.total, self.packed = scratch[:5]
        super().__init__(place, *scratch[5:])

    def give(self, name, src, dst):
        self.flying.setdefault(name, []).append(self.copy(src, dst, self.place.sibling()))

    def give_features(self, name, slot, values, kept):
        core, half = self.place.core, D // 2

        def feature(n):
            m = n & (half - 1)
            owner = jnp.where(n < half, core, 1 - core)
            return ((m >> 5) * CORES + owner) * 32 + (m & 31)

        moved = dot_nt(one_hot(D, D, feature), values).astype(B16)
        kept[0] = moved[0:half]
        self.out[slot] = moved[half:D]
        self.give(name, self.out.at[slot], kept.at[1])


def gather_scratch():
    copies = 2 * (2 * XS - 1)
    return [
        pltpu.VMEM((2 * XS, MERGED, D2), B16),
        pltpu.VMEM((2 * XS, MERGED, D // 2), B16),
        pltpu.VMEM((XS, CORES, MERGED, D // 2), B16),
        pltpu.SemaphoreType.DMA((copies,)),
        pltpu.SemaphoreType.DMA((copies,)),
    ]


class Gather(Copies):
    def __init__(self, place, scratch):
        self.grad, self.hidden, self.hidden_parts = scratch[:3]
        super().__init__(place, *scratch[3:])

    def around(self):
        return [(k, f) for k in range(XS) for f in range(2) if (k, f) != (0, 0)]

    def start_grads(self):
        place = self.place
        self.flying["grads"] = []
        for k, f in self.around():
            pair = place.at(x=place.x_step(k), core=place.core_step(f))
            self.flying["grads"].append(
                self.copy(self.grad.at[0], self.grad.at[2 * k + f], pair)
            )

    def start_hidden(self, hidden):
        place = self.place
        for x in range(XS):
            for ylo in range(YLO):
                for core in range(CORES):
                    start = ((x * YLO + ylo) * CORES + core) * 128
                    self.hidden_parts[x, core, :, 128 * ylo : 128 * (ylo + 1)] = hidden[
                        :, start : start + 128
                    ]
        self.flying["hidden"] = []
        for k, f in self.around():
            x, core = place.x_step(k), place.core_step(f)
            self.flying["hidden"].append(
                self.copy(
                    self.hidden_parts.at[x, core],
                    self.hidden.at[2 * k + f],
                    place.at(x=x, core=core),
                )
            )
        self.hidden[0] = self.hidden_parts[place.x, place.core]

    def form(self, grads_t, path):
        self.wait("hidden")
        hidden = self.hidden[...].reshape(2 * XS * MERGED, D // 2)
        for yhi in range(YHI):
            block = dot(grads_t[pl.ds(D * yhi, D)], hidden).astype(B16)
            for ylo in range(YLO):
                path.sum[ylo, yhi] = block[:, 128 * ylo : 128 * (ylo + 1)]


def iota(shape, dim):
    return lax.broadcasted_iota(jnp.int32, shape, dim)


def one_hot(rows, cols, index):
    place = index(iota((rows, 1), 0))
    return jnp.where(iota((rows, cols), 1) == place, 1.0, 0.0).astype(B16)


def dot(a, b):
    return jnp.dot(a, b, preferred_element_type=F32)


def dot_nt(a, b):
    return lax.dot_general(a, b, (((1,), (1,)), ((), ())), preferred_element_type=F32)


def dot_tn(a, b):
    return lax.dot_general(a, b, (((0,), (0,)), ((), ())), preferred_element_type=F32)


def rows_at(n):
    return n >> 5, n & 31


def rows_index(i, j):
    return i * COLS + j


def merge_at(n):
    part, r, c = n >> 6, (n >> 4) & 3, n & 15
    return 2 * r + (part & 1), 2 * c + (part >> 1)


def merge_index(i, j):
    return (((j & 1) * 2 + (i & 1)) << 6) + ((i >> 1) << 4) + (j >> 1)


def window_at(n):
    return (n >> 3) & 7, ((n >> 6) << 3) + (n & 7)


def window_index(i, j):
    return ((j >> 3) << 6) + (i << 3) + (j & 7)


def fringe_at(n, deep):
    side = n < 64 * deep
    strip = n < 64 * deep + 64
    m = n & 31
    i_side = (n >> 5) + jnp.where(n < 32 * deep, 0, ROWS - 2 * deep)
    i = jnp.where(side, i_side, jnp.where(strip, m >> 2, ((n & 15) >> 2) + 4 * ((n >> 5) & 1)))
    last = jnp.where(strip, (n >> 5) & 1, (n >> 4) & 1)
    j = jnp.where(side, m, (n & 3) + last * (COLS - 4))
    return i, j


def around_index(index, i, j, deep):
    up, down, left, right = i < 0, i >= ROWS, j < 0, j >= COLS
    col4 = jnp.where(left, j + 4, j - COLS)
    north = up | down
    side = north & ~(left | right)
    strip = (left | right) & ~north
    corner = north & (left | right)
    at = index(i, j)
    row = jnp.where(up, i + 2 * deep, i - ROWS)
    at = jnp.where(side, CELLS + row * COLS + j, at)
    at = jnp.where(strip, CELLS + 64 * deep + jnp.where(left, 32, 0) + i * 4 + col4, at)
    base = CELLS + 64 * deep + 64 + jnp.where(up, 32, 0) + jnp.where(left, 16, 0)
    row4 = jnp.where(up, i + 4, i - ROWS)
    return jnp.where(corner, base + row4 * 4 + col4, at)


def normalize(values):
    center = values - jnp.mean(values, axis=-1, keepdims=True)
    inverse = lax.rsqrt(jnp.mean(center * center, axis=-1, keepdims=True) + EPSILON)
    return center * inverse, inverse


def fringe_size(deep):
    return 64 * deep + 128


def fringes(deep):
    rows, base = 32 * deep, 64 * deep
    return (
        (0, rows, -1, 0),
        (rows, rows, 1, 0),
        (base, 32, 0, -1),
        (base + 32, 32, 0, 1),
        (base + 64, 16, -1, -1),
        (base + 80, 16, -1, 1),
        (base + 96, 16, 1, -1),
        (base + 112, 16, 1, 1),
    )


def around_scratch(deep):
    return [
        pltpu.VMEM((CELLS + fringe_size(deep), D), B16),
        pltpu.VMEM((fringe_size(deep), D), B16),
        pltpu.SemaphoreType.DMA((8,)),
        pltpu.SemaphoreType.DMA((8,)),
    ]


class Around(Copies):
    def __init__(self, place, deep, scratch):
        self.block, self.fringe = scratch[:2]
        self.deep = deep
        super().__init__(place, *scratch[2:])

    def pick(self, values, picks):
        self.fringe[...] = dot(picks, values).astype(B16)

    def start(self, values):
        self.flying["fringe"] = [
            self.copy(
                self.fringe.at[pl.ds(offset, size)],
                self.block.at[pl.ds(CELLS + offset, size)],
                self.place.beside(dlat, dlon),
            )
            for offset, size, dlat, dlon in fringes(self.deep)
        ]
        self.block[pl.ds(0, CELLS)] = values

    def get(self, picks):
        self.wait("fringe")
        return dot(picks, self.block[...])


def section_kernel(
    deep,
    shift,
    tokens_hbm,
    skip_grad_hbm,
    merged_grad_hbm,
    w_qkv_hbm,
    w_proj_hbm,
    w_merge_hbm,
    skip_out,
    merged_out,
    input_grad,
    sum_merge,
    sum_fine,
    tokens,
    skip_grad,
    w_qkv,
    w_proj,
    w_merge,
    load,
    to_back,
    to_windows,
    to_output,
    pick_window,
    pick_merge,
    normed,
    packed,
    probs,
    attended,
    window_total,
    packed_grad,
    merged_hidden,
    total_grad,
    grads_t,
    *scratch,
):
    place = Place()
    partners = place.partners()
    greet(partners)
    rounds = [Around(place, deep, scratch[4 * n : 4 * n + 4]) for n in range(4)]
    scratch = scratch[16:]
    factors = Gather(place, scratch[:5])
    merge_sum = PathXY(place, scratch[5:9])
    proj_sum = PathXY(place, scratch[9:15])
    qkv_sums = PathXY(place, scratch[15:21]), PathYX(place, scratch[21:27])
    merge_last = Last(place, scratch[27:31])
    fine_last = Last(place, scratch[31:35])
    share = Share(place, scratch[35:42])
    merged_grad = factors.grad.at[0]
    loads = {}
    for n, (name, src, dst) in enumerate(
        (
            ("tokens", tokens_hbm, tokens),
            ("merged_grad", merged_grad_hbm, merged_grad),
            ("w_qkv", w_qkv_hbm, w_qkv),
            ("skip_grad", skip_grad_hbm, skip_grad),
            ("w_proj", w_proj_hbm, w_proj),
            ("w_merge", w_merge_hbm, w_merge),
        )
    ):
        loads[name] = pltpu.make_async_copy(src, dst, load.at[n])
        loads[name].start()

    a, b = shift[0], shift[1]
    down = jnp.where(a >= WIN // 2, a - WIN, a)
    right = jnp.where(b >= WIN // 2, b - WIN, b)

    def picker(index):
        return one_hot(fringe_size(deep), CELLS, lambda n: index(*fringe_at(n, deep)))

    def shifted(at, index, sign):
        def source(n):
            i, j = at(n)
            return around_index(index, i + sign * down, j + sign * right, deep)

        return one_hot(CELLS, CELLS + fringe_size(deep), source)

    from_tokens = shifted(window_at, rows_index, 1)
    pick_tokens = picker(rows_index)
    loads["tokens"].wait()
    rounds[0].pick(tokens[...], pick_tokens)
    await_greetings(partners)
    rounds[0].start(tokens[...])
    loads["merged_grad"].wait()
    factors.start_grads()

    to_back[...] = shifted(merge_at, window_index, -1)
    to_windows[...] = shifted(window_at, merge_index, 1)
    to_output[...] = shifted(rows_at, window_index, -1)
    pick_window[...] = picker(window_index)
    pick_merge[...] = picker(merge_index)
    to_merged = one_hot(CELLS, CELLS, lambda n: rows_index(*merge_at(n)))
    to_rows = one_hot(CELLS, CELLS, lambda n: merge_index(*rows_at(n)))
    own_tokens = dot(to_merged, tokens[...])
    loads["skip_grad"].wait()
    own_skip = dot(to_merged, skip_grad[...])
    loads["w_qkv"].wait()

    values, inverse = normalize(rounds[0].get(from_tokens))
    normed[...] = values
    hidden = values.astype(B16)
    for n in range(3):
        columns = pl.ds(D * n, D)
        packed[:, columns] = dot(hidden, w_qkv[:, columns]).astype(B16)

    head_mask = (iota((4 * 64, 128), 0) >> 6) == (iota((4 * 64, 128), 1) >> 5)
    head_one = jnp.where(head_mask, 1.0, 0.0)
    head_b16 = head_one.astype(B16)

    def expand(values):
        return jnp.concatenate([values] * 4, axis=0) * head_b16

    def fold(values):
        kept = values * head_one
        return (kept[0:64] + kept[64:128]) + (kept[128:192] + kept[192:256])

    def lanes(n, g):
        return pl.ds(D * n + 128 * g, 128)

    key_row = down + ((iota((64, 1), 0) >> 3) & 7)
    query_row = down + ((iota((1, 256), 1) >> 3) & 7)
    key_away = (key_row < 0) | (key_row >= ROWS)
    query_away = (query_row < 0) | (query_row >= ROWS)
    pole = place.lat == jnp.where(a >= WIN // 2, 0, YHI * ZS - 1)
    apart = jnp.where(key_away, 1, 0) != jnp.where(query_away, 1, 0)
    bias = jnp.where(apart, jnp.where(pole, NEGATIVE, 0.0), 0.0)

    def forward(w, carry):
        rows = pl.ds(pl.multiple_of(w * 64, 64), 64)
        for g in range(4):
            queries = expand(packed[rows, lanes(0, g)])
            scores = dot_nt(packed[rows, lanes(1, g)], queries) * FACTOR + bias
            raised = jnp.exp(scores - jnp.max(scores, axis=0, keepdims=True))
            prob = raised * (1.0 / jnp.sum(raised, axis=0, keepdims=True))
            probs[w, g] = prob
            output = dot_tn(prob.astype(B16), packed[rows, lanes(2, g)])
            attended[rows, pl.ds(128 * g, 128)] = fold(output).astype(B16)
        return carry

    lax.fori_loop(0, WINDOWS, forward, 0)
    rounds[1].pick(attended[...], pick_window[...])
    rounds[1].start(attended[...])

    loads["w_proj"].wait()
    loads["w_merge"].wait()
    merged_back = [
        dot_nt(merged_grad[...], w_merge[pl.ds(D * part, D)]) for part in range(4)
    ]
    share.give_features("hidden", 0, hidden, share.hidden)
    share.give_features("attended", 1, attended[...], share.attended)

    own_attended = rounds[1].get(to_back[...]).astype(B16)
    own_out = (own_tokens + dot(own_attended, w_proj[...])).astype(B16)
    merged_in = own_out.astype(F32)
    quarters = [merged_in[MERGED * n : MERGED * (n + 1)] for n in range(4)]
    wide = 1.0 / (4 * D)

    def mean(values):
        return sum(jnp.sum(v, axis=-1, keepdims=True) for v in values) * wide

    center_at = mean(quarters)
    centers = [q - center_at for q in quarters]
    merged_inverse = lax.rsqrt(mean([c * c for c in centers]) + EPSILON)
    merged_normed = [c * merged_inverse for c in centers]
    back_mean = mean(merged_back)
    back_dot = mean([g * n for g, n in zip(merged_back, merged_normed)])
    for n in range(4):
        rows = pl.ds(MERGED * n, MERGED)
        merged_hidden[:, pl.ds(D * n, D)] = merged_normed[n].astype(B16)
        delta = merged_inverse * (merged_back[n] - back_mean - merged_normed[n] * back_dot)
        total_grad[rows] = (own_skip[MERGED * n : MERGED * (n + 1)] + delta).astype(B16)
    rounds[2].pick(total_grad[...], pick_merge[...])
    rounds[2].start(total_grad[...])
    factors.start_hidden(merged_hidden)

    skip_out[...] = dot(to_rows, own_out).astype(B16)
    merged_out[...] = dot(merged_hidden[...], w_merge[...]).astype(B16)
    factors.wait("grads")
    grads_t[...] = factors.grad[...].reshape(2 * XS * MERGED, D2).T

    window_total[...] = rounds[2].get(to_windows[...]).astype(B16)
    share.give("total", window_total, share.total)
    attended[...] = dot_nt(window_total[...], w_proj[...]).astype(B16)

    def backward(w, carry):
        rows = pl.ds(pl.multiple_of(w * 64, 64), 64)
        for g in range(4):
            queries = expand(packed[rows, lanes(0, g)])
            upstream = expand(attended[rows, pl.ds(128 * g, 128)])
            key_rows, value_rows = packed[rows, lanes(1, g)], packed[rows, lanes(2, g)]
            prob = probs[w, g]
            prob_grad = dot_nt(value_rows, upstream)
            total = jnp.sum(prob * prob_grad, axis=0, keepdims=True)
            score_grad = (prob * (prob_grad - total) * FACTOR).astype(B16)
            packed_grad[rows, lanes(0, g)] = fold(dot_tn(score_grad, key_rows)).astype(B16)
            packed_grad[rows, lanes(1, g)] = dot(score_grad, queries).astype(B16)
            packed_grad[rows, lanes(2, g)] = dot(prob.astype(B16), upstream).astype(B16)
        return carry

    def give_packed(part):
        rows = pl.ds(CELLS // 2 * part, CELLS // 2)
        share.give("packed", packed_grad.at[rows], share.packed.at[rows])

    def give_packed(part):
        rows = pl.ds(CELLS // 2 * part, CELLS // 2)
        share.give("packed", packed_grad.at[rows], share.packed.at[rows])

    factors.form(grads_t, merge_sum)
    merge_sum.start_second()
    lax.fori_loop(0, WINDOWS // 2, backward, 0)
    give_packed(0)
    share.wait("attended")
    share.wait("total")
    block = dot(share.attended[0], window_total[...]) + dot(share.attended[1], share.total[...])
    block = block.astype(B16)
    for yhi in range(YHI):
        for h in range(2):
            start = 256 * yhi + 128 * h
            proj_sum.parts[:, :, yhi, pl.ds(32 * h, 32)] = block[:, start : start + 128].reshape(
                XS, YLO, 32, 128
            )
    proj_sum.start_first()
    lax.fori_loop(WINDOWS // 2, WINDOWS, backward, 0)
    give_packed(1)

    hidden_grad = dot_nt(packed_grad[...], w_qkv[...])
    proj_sum.add_first()
    proj_sum.start_second()
    share.wait("hidden")
    share.wait("packed")
    for h in range(2):
        for yhi in range(YHI):
            columns = pl.ds(768 * yhi + 384 * h, 384)
            block = dot(share.hidden[0], packed_grad[:, columns])
            block = (block + dot(share.hidden[1], share.packed[:, columns])).astype(B16)
            for m in range(3):
                qkv_sums[h].parts[:, :, yhi, pl.ds(32 * m, 32)] = block[
                    :, 128 * m : 128 * (m + 1)
                ].reshape(XS, YLO, 32, 128)
        qkv_sums[h].start_first()
    merge_last.column[...] = merge_sum.add_second().reshape(ZS, 64, 128)
    merge_last.start()

    window_input = window_total[...].astype(F32) + inverse * (
        hidden_grad
        - jnp.mean(hidden_grad, axis=-1, keepdims=True)
        - normed[...] * jnp.mean(hidden_grad * normed[...], axis=-1, keepdims=True)
    )
    window_input = window_input.astype(B16)
    rounds[3].pick(window_input, pick_window[...])

    widen_fine = one_hot(384, 512, lambda n: (n // 96) * 128 + n % 96)
    widen_proj = one_hot(128, 512, lambda n: (n >> 5) * 128 + 96 + (n & 31))
    for path in qkv_sums:
        path.add_first()
        path.start_second()
    rounds[3].start(window_input)
    proj_total = proj_sum.add_second()
    proj_wide = [dot(proj_total[32 * h : 32 * (h + 1)], widen_proj) for h in range(2)]
    for h, path in enumerate(qkv_sums):
        total = path.add_second()
        wide_rows = jnp.concatenate([total[32 * m : 32 * (m + 1)] for m in range(3)], axis=1)
        block = (dot(wide_rows, widen_fine) + proj_wide[h]).astype(B16)
        for m in range(HALF):
            fine_last.column[HALF * h + m] = block[:, 128 * m : 128 * (m + 1)]
    fine_last.start()
    merge_last.add(sum_merge)
    input_grad[...] = rounds[3].get(to_output[...]).astype(B16)
    fine_last.add(sum_fine)


def finish_kernel(sum_merge, sum_fine, *refs):
    for src, dst in zip(refs[:3], refs[3:6]):
        dst[...] = src[...]
    dw_qkv, dw_proj, dw_merge = refs[6:]
    dw_qkv[...] = sum_fine[:, 0:96]
    dw_proj[...] = sum_fine[:, 96:128]
    dw_merge[...] = sum_merge[...]


def section(deep, *args):
    vmem, smem = pltpu.VMEM, pltpu.SMEM
    inside = pl.BlockSpec(memory_space=vmem)
    outside = pl.BlockSpec(memory_space=pl.ANY)
    shape = jax.ShapeDtypeStruct
    big = [shape((CELLS, D), B16), shape((MERGED, D2), B16), shape((CELLS, D), B16)]
    fringe = fringe_size(deep)
    return pl.pallas_call(
        functools.partial(section_kernel, deep),
        out_shape=big + [shape((64, 128), F32), shape((32, 128), F32)],
        in_specs=[pl.BlockSpec(memory_space=smem)] + [outside] * 6,
        out_specs=[inside] * 5,
        scratch_shapes=[
            vmem((CELLS, D), B16),
            vmem((CELLS, D), B16),
            vmem((D, 3 * D), B16),
            vmem((D, D), B16),
            vmem((4 * D, D2), B16),
            pltpu.SemaphoreType.DMA((6,)),
            vmem((CELLS, CELLS + fringe), B16),
            vmem((CELLS, CELLS + fringe), B16),
            vmem((CELLS, CELLS + fringe), B16),
            vmem((fringe, CELLS), B16),
            vmem((fringe, CELLS), B16),
            vmem((CELLS, D), F32),
            vmem((CELLS, 3 * D), B16),
            vmem((WINDOWS, 4, 64, 256), F32),
            vmem((CELLS, D), B16),
            vmem((CELLS, D), B16),
            vmem((CELLS, 3 * D), B16),
            vmem((MERGED, 4 * D), B16),
            vmem((CELLS, D), B16),
            vmem((D2, 2 * XS * MERGED), B16),
        ]
        + around_scratch(deep) * 4
        + gather_scratch()
        + path_scratch(512, (False, 1), (YLO, YHI))
        + path_scratch(64, (True, XS), (YLO, YHI))
        + path_scratch(96, (True, XS), (YLO, YHI))
        + path_scratch(96, (True, YS), (XS,))
        + last_scratch(64)
        + last_scratch(32)
        + share_scratch(),
        compiler_params=pltpu.CompilerParams(
            collective_id=deep, has_side_effects=True, vmem_limit_bytes=56 * 2**20
        ),
    )(*args)


def on_device(tokens, w_qkv, w_proj, w_merge, skip_grad, merged_grad, window_shift):
    inside = pl.BlockSpec(memory_space=pltpu.VMEM)
    shape = jax.ShapeDtypeStruct
    big = [shape((CELLS, D), B16), shape((MERGED, D2), B16), shape((CELLS, D), B16)]
    args = (
        window_shift,
        tokens.reshape(CELLS, D),
        skip_grad.reshape(CELLS, D),
        merged_grad.reshape(MERGED, D2),
        w_qkv,
        w_proj,
        w_merge,
    )
    shift = window_shift[0]
    rows = jnp.minimum(shift, WIN - shift)
    skip_out, merged_out, input_grad, sum_merge, sum_fine = lax.switch(
        jnp.minimum(rows, 3) - 1, [functools.partial(section, deep) for deep in (1, 2, 4)], *args
    )
    skip_out, merged_out, input_grad, dw_qkv, dw_proj, dw_merge = pl.pallas_call(
        finish_kernel,
        out_shape=big + [shape((32, 96), F32), shape((32, 32), F32), shape((64, 128), F32)],
        in_specs=[inside] * 5,
        out_specs=[inside] * 6,
    )(sum_merge, sum_fine, skip_out, merged_out, input_grad)
    return (
        skip_out.reshape(ROWS, COLS, D),
        merged_out.reshape(ROWS // 2, COLS // 2, D2),
        input_grad.reshape(ROWS, COLS, D),
        dw_qkv,
        dw_proj,
        dw_merge.T,
    )


def solution(mesh):
    in_specs = (
        P("lat", "lon", None),
        P(),
        P(),
        P(),
        P("lat", "lon", None),
        P("lat", "lon", None),
        P(),
    )
    out_specs = (
        P("lat", "lon", None),
        P("lat", "lon", None),
        P("lat", "lon", None),
        P("lon", "lat"),
        P("lon", "lat"),
        P("lon", "lat"),
    )
    return jax.shard_map(
        on_device, mesh=mesh, in_specs=in_specs, out_specs=out_specs, check_vma=False
    )
```

time: 75.8 us -> 70.8 us (0.934)
  Pallas kernels: 73.8 us -> 67 us
  between operations: 0.64 us -> 1.94 us
    pallas_call x1, Pallas kernels: 71.8 us -> 66.2 us  [section(): pl.pallas_call(functools.partial(section_kernel, deep), out_shape=big + [...]
    pallas_call x1, Pallas kernels: 1.98 us -> 0.85 us  [on_device(): pl.pallas_call(finish_kernel, out_shape=big + [shape((32, 96), F32), shap...]
where the time goes in v4:
time: 70.8 us; the launch traced here: 69.7 us
  Pallas kernels  67 us (95%)
  between operations  1.94 us (3%)
    pallas_call x1, Pallas kernels, section(): pl.pallas_call(functools.partial(section_kernel, deep), out_shape=big + [...  66.2 us

profile of v4, /device:TPU:4, one launch (start us, length us, event | category | flops | bytes accessed | tf_op | source)
XLA Modules:
  0.0 69.7 jit_solution(1541598399861205904)
XLA Ops:
  1.9 66.9 %conditional.1 = ((bf16[256,512]{1,0:T(8,128)(2,1)S(1)}, bf16[64,1024]{1,0:T(8,128)(2,1)S(1)}, bf16[256,512]{1,0:T(8,128)(2,1)S(1)}, f32[64,128]{1,0:T(8,128)S(1)}, f32[32,128]{1,0:T(8,128)S(1)})) conditional(s32[]{:T(128)} %clamp.3, (s32[2]{0:T(128)}, bf16[256,512]{1,0:T(8,128)(2,1)}, bf16[256,512]{1,0:T(8,128)(2,1)}, ...), branch_computations={%region_0.0_spmd, %region_1.0_spmd, %region_2.0_spmd} | conditional | bytes 8 | solution.py:825
  2.4 66.2 %branch_2_fun.1 = (bf16[256,512]{1,0:T(8,128)(2,1)S(1)}, bf16[64,1024]{1,0:T(8,128)(2,1)S(1)}, bf16[256,512]{1,0:T(8,128)(2,1)S(1)}, f32[64,128]{1,0:T(8,128)S(1)}, f32[32,128]{1,0:T(8,128)S(1)}) custom-call(s32[2]{0:T(128)} %get-tuple-element.56.shift, bf16[256,512]{1,0:T(8,128)(2,1)} %get-tuple-element.57.tokens_hbm, ...), custom_call_target="tpu_custom_call" | custom-call | tf_op jit(solution)/shard_map/cond/branch_2_fun/pallas_call | solution.py:768
  68.8 0.9 %shard_map.118 = (bf16[256,512]{1,0:T(8,128)(2,1)}, bf16[64,1024]{1,0:T(8,128)(2,1)}, bf16[256,512]{1,0:T(8,128)(2,1)}, f32[32,96]{1,0:T(8,128)}, f32[32,32]{1,0:T(8,128)}, /*index=5*/f32[64,128]{1,0:T(8,128)}) custom-call(f32[64,128]{1,0:T(8,128)S(1)} %get-tuple-element.80.sum_merge, f32[32,128]{1,0:T(8,128)S(1)} %get-tuple-element.81.sum_fine, ...), custom_call_target="tpu_custom_call" | custom-call | tf_op jit(solution)/shard_map/pallas_call | solution.py:828

commit v5 on v4

--- a/solution.py
+++ b/solution.py
@@ -341,10 +341,15 @@
     def form(self, grads_t, path):
         self.wait("hidden")
         hidden = self.hidden[...].reshape(2 * XS * MERGED, D // 2)
-        for yhi in range(YHI):
-            block = dot(grads_t[pl.ds(D * yhi, D)], hidden).astype(B16)
+
+        def body(yhi, carry):
+            rows = pl.ds(pl.multiple_of(D * yhi, D), D)
+            block = dot(grads_t[rows], hidden).astype(B16)
             for ylo in range(YLO):
                 path.sum[ylo, yhi] = block[:, 128 * ylo : 128 * (ylo + 1)]
+            return carry
+
+        lax.fori_loop(0, YHI, body, 0)
 
 
 def iota(shape, dim):
@@ -512,6 +517,8 @@
     merged_hidden,
     total_grad,
     grads_t,
+    own_part,
+    back,
     *scratch,
 ):
     place = Place()
@@ -579,9 +586,13 @@
     values, inverse = normalize(rounds[0].get(from_tokens))
     normed[...] = values
     hidden = values.astype(B16)
-    for n in range(3):
-        columns = pl.ds(D * n, D)
+
+    def project(n, carry):
+        columns = pl.ds(pl.multiple_of(D * n, D), D)
         packed[:, columns] = dot(hidden, w_qkv[:, columns]).astype(B16)
+        return carry
+
+    lax.fori_loop(0, 3, project, 0)
 
     head_mask = (iota((4 * 64, 128), 0) >> 6) == (iota((4 * 64, 128), 1) >> 5)
     head_one = jnp.where(head_mask, 1.0, 0.0)
@@ -617,19 +628,24 @@
             attended[rows, pl.ds(128 * g, 128)] = fold(output).astype(B16)
         return carry
 
-    lax.fori_loop(0, WINDOWS, forward, 0)
+    lax.fori_loop(0, WINDOWS, forward, 0, unroll=2)
     rounds[1].pick(attended[...], pick_window[...])
     rounds[1].start(attended[...])
 
     loads["w_proj"].wait()
     loads["w_merge"].wait()
-    merged_back = [
-        dot_nt(merged_grad[...], w_merge[pl.ds(D * part, D)]) for part in range(4)
-    ]
+
+    def merge_back(part, carry):
+        rows = pl.ds(pl.multiple_of(D * part, D), D)
+        back[part] = dot_nt(merged_grad[...], w_merge[rows])
+        return carry
+
+    lax.fori_loop(0, 4, merge_back, 0)
     share.give_features("hidden", 0, hidden, share.hidden)
     share.give_features("attended", 1, attended[...], share.attended)
 
     own_attended = rounds[1].get(to_back[...]).astype(B16)
+    merged_back = [back[part] for part in range(4)]
     own_out = (own_tokens + dot(own_attended, w_proj[...])).astype(B16)
     merged_in = own_out.astype(F32)
     quarters = [merged_in[MERGED * n : MERGED * (n + 1)] for n in range(4)]
@@ -687,7 +703,7 @@
 
     factors.form(grads_t, merge_sum)
     merge_sum.start_second()
-    lax.fori_loop(0, WINDOWS // 2, backward, 0)
+    lax.fori_loop(0, WINDOWS // 2, backward, 0, unroll=2)
     give_packed(0)
     share.wait("attended")
     share.wait("total")
@@ -700,27 +716,38 @@
                 XS, YLO, 32, 128
             )
     proj_sum.start_first()
-    lax.fori_loop(WINDOWS // 2, WINDOWS, backward, 0)
+    lax.fori_loop(WINDOWS // 2, WINDOWS, backward, 0, unroll=2)
     give_packed(1)
 
-    hidden_grad = dot_nt(packed_grad[...], w_qkv[...])
-    proj_sum.add_first()
-    proj_sum.start_second()
     share.wait("hidden")
+
+    def form_own(n, carry):
+        columns = pl.ds(pl.multiple_of(D * n, D), D)
+        own_part[:, columns] = dot(share.hidden[0], packed_grad[:, columns])
+        return carry
+
+    lax.fori_loop(0, 3, form_own, 0)
     share.wait("packed")
     for h in range(2):
-        for yhi in range(YHI):
-            columns = pl.ds(768 * yhi + 384 * h, 384)
-            block = dot(share.hidden[0], packed_grad[:, columns])
-            block = (block + dot(share.hidden[1], share.packed[:, columns])).astype(B16)
+
+        def form_both(yhi, carry):
+            columns = pl.ds(pl.multiple_of(768 * yhi + 384 * h, 128), 384)
+            block = own_part[:, columns] + dot(share.hidden[1], share.packed[:, columns])
+            block = block.astype(B16)
             for m in range(3):
                 qkv_sums[h].parts[:, :, yhi, pl.ds(32 * m, 32)] = block[
                     :, 128 * m : 128 * (m + 1)
                 ].reshape(XS, YLO, 32, 128)
+            return carry
+
+        lax.fori_loop(0, YHI, form_both, 0)
         qkv_sums[h].start_first()
+    proj_sum.add_first()
+    proj_sum.start_second()
     merge_last.column[...] = merge_sum.add_second().reshape(ZS, 64, 128)
     merge_last.start()
 
+    hidden_grad = dot_nt(packed_grad[...], w_qkv[...])
     window_input = window_total[...].astype(F32) + inverse * (
         hidden_grad
         - jnp.mean(hidden_grad, axis=-1, keepdims=True)
@@ -791,6 +818,8 @@
             vmem((MERGED, 4 * D), B16),
             vmem((CELLS, D), B16),
             vmem((D2, 2 * XS * MERGED), B16),
+            vmem((D // 2, 3 * D), F32),
+            vmem((4, MERGED, D), F32),
         ]
         + around_scratch(deep) * 4
         + gather_scratch()

time: 70.8 us -> 68.3 us (0.965)
  Pallas kernels: 67 us -> 64.5 us
    pallas_call x1, Pallas kernels: 66.2 us -> 63.7 us  [section(): pl.pallas_call(functools.partial(section_kernel, deep), out_shape=big + [...]
where the time goes in v5:
time: 68.3 us; the launch traced here: 67.1 us
  Pallas kernels  64.5 us (94%)
  between operations  1.94 us (3%)
  loops' own time  0.69 us (1%)
    pallas_call x1, Pallas kernels, section(): pl.pallas_call(functools.partial(section_kernel, deep), out_shape=big + [...  63.7 us

profile of v5, /device:TPU:4, one launch (start us, length us, event | category | flops | bytes accessed | tf_op | source)
XLA Modules:
  0.0 67.1 jit_solution(14341074123860923658)
XLA Ops:
  1.9 64.4 %conditional.1 = ((bf16[256,512]{1,0:T(8,128)(2,1)S(1)}, bf16[64,1024]{1,0:T(8,128)(2,1)S(1)}, bf16[256,512]{1,0:T(8,128)(2,1)S(1)}, f32[64,128]{1,0:T(8,128)S(1)}, f32[32,128]{1,0:T(8,128)S(1)})) conditional(s32[]{:T(128)} %clamp.3, (s32[2]{0:T(128)}, bf16[256,512]{1,0:T(8,128)(2,1)}, bf16[256,512]{1,0:T(8,128)(2,1)}, ...), branch_computations={%region_0.0_spmd, %region_1.0_spmd, %region_2.0_spmd} | conditional | bytes 8 | solution.py:854
  2.4 63.7 %branch_2_fun.1 = (bf16[256,512]{1,0:T(8,128)(2,1)S(1)}, bf16[64,1024]{1,0:T(8,128)(2,1)S(1)}, bf16[256,512]{1,0:T(8,128)(2,1)S(1)}, f32[64,128]{1,0:T(8,128)S(1)}, f32[32,128]{1,0:T(8,128)S(1)}) custom-call(s32[2]{0:T(128)} %get-tuple-element.56.shift, bf16[256,512]{1,0:T(8,128)(2,1)} %get-tuple-element.57.tokens_hbm, ...), custom_call_target="tpu_custom_call" | custom-call | tf_op jit(solution)/shard_map/cond/branch_2_fun/pallas_call | solution.py:795
  66.3 0.9 %shard_map.118 = (bf16[256,512]{1,0:T(8,128)(2,1)}, bf16[64,1024]{1,0:T(8,128)(2,1)}, bf16[256,512]{1,0:T(8,128)(2,1)}, f32[32,96]{1,0:T(8,128)}, f32[32,32]{1,0:T(8,128)}, /*index=5*/f32[64,128]{1,0:T(8,128)}) custom-call(f32[64,128]{1,0:T(8,128)S(1)} %get-tuple-element.80.sum_merge, f32[32,128]{1,0:T(8,128)S(1)} %get-tuple-element.81.sum_fine, ...), custom_call_target="tpu_custom_call" | custom-call | tf_op jit(solution)/shard_map/pallas_call | solution.py:857
